TPU v7x, 32 devices: a whole 2x2x4 slice. The times are simulated.
32 devices in a mesh: ctx: 8 (over z, x), fsdp: 4 (over y, core).
Axes of the slice: x: 2, y: 2, z: 4, core: 2. Of those that a mesh axis runs over, the one named last changes fastest.
Arguments:
- x_cur: bfloat16 [4, 2048, 2048], P('fsdp', 'ctx'), may hold values from -6 to 6
- x_next: bfloat16 [4, 2048, 2048], P('fsdp', 'ctx'), may hold values from -6 to 6
- cot_cur: bfloat16 [4, 2048, 2048], P('fsdp', 'ctx'), may hold values from -6 to 6
- cot_next: bfloat16 [4, 2048, 2048], P('fsdp', 'ctx'), may hold values from -6 to 6
- w_q: bfloat16 [2048, 1024], P('fsdp')
- w_kv: bfloat16 [2048, 512], P('fsdp')
- w_out: bfloat16 [2048, 1024], P('fsdp'), may hold values from -0.1875 to 0.1875
Outputs:
- x_prev: bfloat16 [4, 2048, 2048], P('fsdp', 'ctx')
- grad_cur: bfloat16 [4, 2048, 2048], P('fsdp', 'ctx')
- grad_weights: float32 [2048, 2560], P(('ctx', 'fsdp'))
All inputs are finite; a program needn't handle non-finite values.
Results may differ from a plain program's by a relative error of at most 0.015.
The roundings to bfloat16 on the way count: a program that leaves them out, or rounds other values in their place, can miss the bound.
Values may be sent and summed in bfloat16 or wider, within the bound.
A program may use at most 192 MiB of HBM per device.

v0:
```python
import math

import jax
import jax.numpy as jnp
from jax import lax
from jax.sharding import PartitionSpec as P

QUERY_HEADS = 8
KEY_VALUE_HEADS = 2
HEAD_SIZE = 128
WINDOW_TOKENS = 1024


EPS = 1e-05


def from_behind(value, axis, steps):
    count = lax.axis_size(axis)
    leading, last = (max(0, -steps), min(count, count - steps))
    return lax.ppermute(value, axis, [(source, source + steps) for source in range(leading, last)])


def normalize(rows):
    values = rows.astype(jnp.float32)
    inv_rms = lax.rsqrt(jnp.mean(values * values, axis=-1, keepdims=True) + EPS)
    return (values * inv_rms, inv_rms)


def head_block(items, allowed):
    quer3, keys2, vals2, grad3 = items
    scale = 1.0 / math.sqrt(HEAD_SIZE)
    scores = jnp.einsum("imd,jd->mij", quer3, keys2, preferred_element_type=jnp.float32) * scale
    scores = jnp.where(allowed[None], scores, -jnp.inf)
    top = jnp.max(scores, axis=-1, keepdims=True)
    expo = jnp.exp(scores - top)
    probs = expo / jnp.sum(expo, axis=-1, keepdims=True)
    probs_low = probs.astype(jnp.bfloat16)
    attended = jnp.einsum("mij,jd->imd", probs_low, vals2, preferred_element_type=jnp.float32)
    grad_probs = jnp.einsum("imd,jd->mij", grad3, vals2, preferred_element_type=jnp.float32)
    delta = jnp.einsum("imd,imd->mi", grad3.astype(jnp.float32), attended)
    grad_scores = (probs * (grad_probs - delta[..., None]) * scale).astype(jnp.bfloat16)
    grad_query = jnp.einsum("mij,jd->imd", grad_scores, keys2, preferred_element_type=jnp.float32)
    key_gradient = jnp.einsum("mij,imd->jd", grad_scores, quer3, preferred_element_type=jnp.float32)
    value_gradient = jnp.einsum("mij,imd->jd", probs_low, grad3, preferred_element_type=jnp.float32)
    return (
        attended.astype(jnp.bfloat16),
        grad_query.astype(jnp.bfloat16),
        key_gradient.astype(jnp.bfloat16),
        value_gradient.astype(jnp.bfloat16),
    )


def window_block(query_rows, key_value_pairs, output_gradient, base):
    window_extent = key_value_pairs.shape[0]
    element_count = query_rows.shape[0]
    query_group = QUERY_HEADS // KEY_VALUE_HEADS
    query_pos = base + jnp.arange(element_count, dtype=jnp.int32)
    key_pos = base - WINDOW_TOKENS + jnp.arange(window_extent, dtype=jnp.int32)
    offset = query_pos[:, None] - key_pos[None, :]
    allowed = (offset >= 0) & (offset < WINDOW_TOKENS) & (key_pos[None, :] >= 0)
    query_grouped = query_rows.reshape(
        element_count, KEY_VALUE_HEADS, query_group, HEAD_SIZE
    ).transpose(1, 0, 2, 3)
    gradient_grouped = output_gradient.reshape(
        element_count, KEY_VALUE_HEADS, query_group, HEAD_SIZE
    ).transpose(1, 0, 2, 3)
    key_tensor = (
        key_value_pairs[:, : KEY_VALUE_HEADS * HEAD_SIZE]
        .reshape(window_extent, KEY_VALUE_HEADS, HEAD_SIZE)
        .transpose(1, 0, 2)
    )
    value_tensor = (
        key_value_pairs[:, KEY_VALUE_HEADS * HEAD_SIZE :]
        .reshape(window_extent, KEY_VALUE_HEADS, HEAD_SIZE)
        .transpose(1, 0, 2)
    )

    def per_head(items):
        return head_block(items, allowed)

    attended, grad_query, key_gradient, value_gradient = lax.map(
        per_head, (query_grouped, key_tensor, value_tensor, gradient_grouped)
    )
    attended = attended.transpose(1, 0, 2, 3).reshape(element_count, QUERY_HEADS * HEAD_SIZE)
    grad_query = grad_query.transpose(1, 0, 2, 3).reshape(element_count, QUERY_HEADS * HEAD_SIZE)
    key_gradient = key_gradient.transpose(1, 0, 2).reshape(
        window_extent, KEY_VALUE_HEADS * HEAD_SIZE
    )
    value_gradient = value_gradient.transpose(1, 0, 2).reshape(
        window_extent, KEY_VALUE_HEADS * HEAD_SIZE
    )
    value_partial_sum = jnp.concatenate([key_gradient, value_gradient], 1)
    return (attended, grad_query, value_partial_sum)


def shards(x_cur, x_next, cot_cur, cot_next, w_q, w_kv, w_out):
    full_q, full_kv, full_out = (
        lax.all_gather(w_q, "fsdp", axis=0, tiled=True),
        lax.all_gather(w_kv, "fsdp", axis=0, tiled=True),
        lax.all_gather(w_out, "fsdp", axis=0, tiled=True),
    )
    seq_count, shard, width = x_cur.shape
    base = lax.axis_index("ctx") * shard
    preds = WINDOW_TOKENS // shard
    normed, inv_rms = normalize(x_cur)
    hidden = normed.astype(jnp.bfloat16)
    query_rows = jnp.einsum(
        "sid,dc->sic", hidden, full_q, preferred_element_type=jnp.float32
    ).astype(jnp.bfloat16)
    key_value_pairs = jnp.einsum(
        "sid,dc->sic", hidden, full_kv, preferred_element_type=jnp.float32
    ).astype(jnp.bfloat16)
    grad_attn = (
        2.0 * jnp.einsum("sid,dc->sic", cot_next, full_out, preferred_element_type=jnp.float32)
    ).astype(jnp.bfloat16)
    earlier = []
    for hop in range(1, preds + 1):
        earlier.append(from_behind(key_value_pairs, "ctx", hop))
    window_keys = jnp.concatenate(earlier[::-1] + [key_value_pairs], axis=1)

    def per_sequence(items):
        q_rows, kv_rows, g_rows = items
        return window_block(q_rows, kv_rows, g_rows, base)

    attended, grad_query, value_partial_sum = lax.map(
        per_sequence, (query_rows, window_keys, grad_attn)
    )
    owned = value_partial_sum[:, WINDOW_TOKENS:].astype(jnp.float32)
    for hop in range(1, preds + 1):
        piece = value_partial_sum[
            :, WINDOW_TOKENS - hop * shard : WINDOW_TOKENS - (hop - 1) * shard
        ]
        owned = owned + from_behind(piece, "ctx", -hop).astype(jnp.float32)
    grad_kv = owned.astype(jnp.bfloat16)
    layer_out = jnp.einsum("sic,dc->sid", attended, full_out, preferred_element_type=jnp.float32)
    x_prev = (x_next.astype(jnp.float32) - 2.0 * layer_out).astype(jnp.bfloat16)
    grad_hidden = jnp.einsum("sic,dc->sid", grad_query, full_q, preferred_element_type=jnp.float32)
    grad_hidden = grad_hidden + jnp.einsum(
        "sic,dc->sid", grad_kv, full_kv, preferred_element_type=jnp.float32
    )
    grad_x = inv_rms * (
        grad_hidden - normed * jnp.mean(grad_hidden * normed, axis=-1, keepdims=True)
    )
    grad_cur = (cot_cur.astype(jnp.float32) + grad_x).astype(jnp.bfloat16)
    hidden_rows = hidden.reshape(seq_count * shard, width)
    cot_rows = cot_next.reshape(seq_count * shard, width)
    left_rows = jnp.concatenate([grad_query, grad_kv], axis=2).reshape(seq_count * shard, -1)
    attended_rows = attended.reshape(seq_count * shard, -1)
    contract_rows = (((0,), (0,)), ((), ()))
    ctx_count = lax.axis_size("ctx")
    fsdp_count = lax.axis_size("fsdp")
    term_in = lax.dot_general(
        hidden_rows, left_rows, contract_rows, preferred_element_type=jnp.float32
    )
    term_out = 2.0 * lax.dot_general(
        cot_rows, attended_rows, contract_rows, preferred_element_type=jnp.float32
    )
    summed = lax.psum_scatter(
        jnp.concatenate([term_in, term_out], axis=1).astype(jnp.bfloat16),
        "ctx",
        scatter_dimension=0,
        tiled=True,
    ).astype(jnp.float32)
    summed = lax.psum_scatter(
        summed.astype(jnp.bfloat16), "fsdp", scatter_dimension=0, tiled=True
    ).astype(jnp.float32)
    token_total = seq_count * shard * ctx_count * fsdp_count
    grad_weights = summed * (1.0 / math.sqrt(token_total))
    return (x_prev, grad_cur, grad_weights)


def solution(mesh):
    in_specs = (
        P("fsdp", "ctx", None),
        P("fsdp", "ctx", None),
        P("fsdp", "ctx", None),
        P("fsdp", "ctx", None),
        P("fsdp", None),
        P("fsdp", None),
        P("fsdp", None),
    )
    out_specs = (P("fsdp", "ctx", None), P("fsdp", "ctx", None), P(("ctx", "fsdp"), None))
    return jax.shard_map(shards, mesh=mesh, in_specs=in_specs, out_specs=out_specs, check_vma=False)
```

profile of v0, /device:TPU:0, one launch (start us, length us, event | category | flops | bytes accessed | tf_op | source)
XLA Modules:
  0.0 432.0 jit_solution(11229307173135875933)
XLA Ops:
  9.8 25.1 %all-gather.4.cloned.1.call-done = bf16[2048,512]{1,0:T(8,128)(2,1)} async-done(((bf16[512,512]{1,0:T(8,128)(2,1)}), bf16[2048,512]{1,0:T(8,128)(2,1)}) %all-gather.4.cloned.1.call-update) | async-done | bytes 2097168 | tf_op jit(solution)/shard_map/all_gather | solution.py:99
  34.9 2.3 fusion.72
  37.2 4.3 %collective-permute-start = (bf16[1,256,512]{2,1,0:T(8,128)(2,1)S(1)}, bf16[1,256,512]{2,1,0:T(8,128)(2,1)S(1)}, u32[]{:S(2)}, u32[]{:S(2)}) collective-permute-start(bf16[1,256,512]{2,1,0:T(8,128)(2,1)S(1)} %fusion.72), channel_id=1, source_target_pairs={{0,16},{4,20},{8,24},{12,28},{1,17},{5,21},{9,25},{13,29},{2,18},{... | collective-permute-start | bytes 786440 | tf_op jit(solution)/shard_map/ppermute | solution.py:20
  41.6 4.3 collective-permute-start.1
  47.3 3.1 collective-permute-start.3
  50.4 3.5 collective-permute-done.1
  53.9 4.9 %collective-permute-done.2 = bf16[1,256,512]{2,1,0:T(8,128)(2,1)S(1)} collective-permute-done((bf16[1,256,512]{2,1,0:T(8,128)(2,1)S(1)}, bf16[1,256,512]{2,1,0:T(8,128)(2,1)S(1)}, u32[]{:S(2)}, u32[]{:S(2)}) %collective-permute-start.2) | collective-permute-done | bytes 262176 | tf_op jit(solution)/shard_map/ppermute | solution.py:20
  61.0 9.9 %all-gather.6.cloned.1.call-done = bf16[2048,1024]{1,0:T(8,128)(2,1)} async-done(((bf16[512,1024]{1,0:T(8,128)(2,1)}), bf16[2048,1024]{1,0:T(8,128)(2,1)}) %all-gather.6.cloned.1.call-update) | async-done | bytes 4194320 | tf_op jit(solution)/shard_map/all_gather | solution.py:98
  71.0 3.5 convolution_convert_fusion.2
  74.8 32.2 %all-gather.8.cloned.1.call-done = bf16[2048,1024]{1,0:T(8,128)(2,1)} async-done(((bf16[512,1024]{1,0:T(8,128)(2,1)}), bf16[2048,1024]{1,0:T(8,128)(2,1)}) %all-gather.8.cloned.1.call-update) | async-done | bytes 4194320 | tf_op jit(solution)/shard_map/all_gather | solution.py:100
  107.1 4.3 fusion.71
  113.9 48.1 %while.29 = (s32[]{:T(128)}, bf16[2,256,4,128]{1,3,2,0:T(8,128)(2,1)}, bf16[2,256,4,128]{1,3,2,0:T(8,128)(2,1)}, bf16[2,1280,128]{1,2,0:T(8,128)(2,1)}, bf16[2,1...) while((s32[]{:T(128)}, ...), condition=%wide.region_4.5_spmd.clone, body=%wide.region_1.4_spmd.clone.sunk | while | flops 2030305536 | bytes 79461984 | solution.py:81
  116.0 5.2 %exponential_reduce_fusion.2 = (f32[4,256]{1,0:T(4,128)S(1)}, f32[4,256,1280]{1,2,0:T(8,128)}) fusion(pred[256,1280]{0,1:T(8,128)(4,1)S(1)} %fusion.132, bf16[2,1280,128]{2,1,0:T(8,128)(2,1)} %get-tuple-element.281, s32[]{:T(128)S(6)} %copy.84, bf16[2,256,4,128]{3,1,2,0:T(8,128)(2,1)} %get-tuple-element.282), kind=kOutput, calls=%fused_computation.9.clone.1 | convolution fusion | flops 340788480 | bytes 6165504 | tf_op jit(solution)/shard_map/while/body/eval_jaxpr/while/body/eval_jaxpr/sub | solution.py:35
  121.3 4.0 fusion.133
  125.3 1.9 fusion.138
  128.7 4.0 fusion.136
  132.9 2.7 fusion.139
  140.1 5.2 %exponential_reduce_fusion.2 = (f32[4,256]{1,0:T(4,128)S(1)}, f32[4,256,1280]{1,2,0:T(8,128)}) fusion(pred[256,1280]{0,1:T(8,128)(4,1)S(1)} %fusion.132, bf16[2,1280,128]{2,1,0:T(8,128)(2,1)} %get-tuple-element.281, s32[]{:T(128)S(6)} %copy.84, bf16[2,256,4,128]{3,1,2,0:T(8,128)(2,1)} %get-tuple-element.282), kind=kOutput, calls=%fused_computation.9.clone.1 | convolution fusion | flops 340788480 | bytes 6165504 | tf_op jit(solution)/shard_map/while/body/eval_jaxpr/while/body/eval_jaxpr/sub | solution.py:35
  145.3 4.0 fusion.133
  149.3 1.9 fusion.138
  152.7 4.0 fusion.136
  156.9 2.7 fusion.139
  170.2 8.9 %collective-permute-done.4 = bf16[1,256,512]{1,2,0:T(8,128)(2,1)S(1)} collective-permute-done((bf16[1,256,512]{1,2,0:T(8,128)(2,1)S(1)}, bf16[1,256,512]{1,2,0:T(8,128)(2,1)S(1)}, u32[]{:S(2)}, u32[]{:S(2)}) %collective-permute-start.4) | collective-permute-done | bytes 262176 | tf_op jit(solution)/shard_map/ppermute | solution.py:20
  179.1 14.2 %collective-permute-done.7 = bf16[1,256,512]{1,2,0:T(8,128)(2,1)S(1)} collective-permute-done((bf16[1,256,512]{1,2,0:T(8,128)(2,1)S(1)}, bf16[1,256,512]{1,2,0:T(8,128)(2,1)S(1)}, u32[]{:S(2)}, u32[]{:S(2)}) %collective-permute-start.7) | collective-permute-done | bytes 262176 | tf_op jit(solution)/shard_map/ppermute | solution.py:20
  193.4 2.9 convolution_convert_fusion.1
  196.4 12.7 %pad_maximum_fusion = bf16[2048,2560]{0,1:T(8,128)(2,1)} fusion(bf16[2048,1024]{0,1:T(8,128)(2,1)S(1)} %fusion.57, bf16[2048,1536]{0,1:T(8,128)(2,1)S(1)} %convolution_convert_fusion.1), kind=kLoop, calls=%fused_computation.63 | loop fusion | flops 20971520 | bytes 20971520 | tf_op jit(solution)/shard_map/concatenate | solution.py:159
  209.1 185.5 %reduce-scatter.5.cloned.1.call-done = bf16[256,2560]{0,1:T(8,128)(2,1)} async-done(((bf16[2048,2560]{0,1:T(8,128)(2,1)}), bf16[256,2560]{0,1:T(8,128)(2,1)}) %reduce-scatter.5.cloned.1.call-update) | async-done | bytes 1310736 | tf_op jit(solution)/shard_map/reduce_scatter | solution.py:158
  394.6 2.4 copy.54
  397.1 3.8 fusion.88
  401.1 2.3 fusion.64
  404.7 1.6 fusion.69
  406.3 16.6 %reduce-scatter.7.cloned.1.call-done = bf16[64,2560]{1,0:T(8,128)(2,1)} async-done(((bf16[256,2560]{1,0:T(8,128)(2,1)}), bf16[64,2560]{1,0:T(8,128)(2,1)}) %reduce-scatter.7.cloned.1.call-update) | async-done | bytes 327696
  (116 shorter events, 33.5 us)
Async XLA Ops:
  7.2 99.9 %copy-start = (bf16[1,256,2048]{2,1,0:T(8,128)(2,1)S(1)}, bf16[1,256,2048]{2,1,0:T(8,128)(2,1)}, u32[]{:S(2)}) copy-start(bf16[1,256,2048]{2,1,0:T(8,128)(2,1)} %param.12) | copy-start | bytes 3145732
  7.2 2.3 copy-start.2
  7.2 27.7 %all-gather.4.cloned.1.call-start = ((), (), s32[]{:S(2)}) async-start(), calls=%async_computation.2 | async-start | bytes 2621440 | tf_op jit(solution)/shard_map/all_gather | solution.py:99
  7.9 63.1 %all-gather.6.cloned.1.call-start = ((), (), s32[]{:S(2)}) async-start(), calls=%async_computation.3 | async-start | bytes 5242880 | tf_op jit(solution)/shard_map/all_gather | solution.py:98
  8.7 98.4 %all-gather.8.cloned.1.call-start = ((), (), s32[]{:S(2)}) async-start(), calls=%async_computation.4 | async-start | bytes 5242880 | tf_op jit(solution)/shard_map/all_gather | solution.py:100
  9.4 385.1 %reduce-scatter.5.cloned.1.call-start = ((), (), s32[]{:S(2)}) async-start(), calls=%async_computation.5 | async-start | bytes 11796480 | tf_op jit(solution)/shard_map/reduce_scatter | solution.py:158
  37.2 13.2 %collective-permute-start = (bf16[1,256,512]{2,1,0:T(8,128)(2,1)S(1)}, bf16[1,256,512]{2,1,0:T(8,128)(2,1)S(1)}, u32[]{:S(2)}, u32[]{:S(2)}) collective-permute-start(bf16[1,256,512]{2,1,0:T(8,128)(2,1)S(1)} %fusion.72), channel_id=1, source_target_pairs={{0,16},{4,20},{8,24},{12,28},{1,17},{5,21},{9,25},{13,29},{2,18},{... | collective-permute-start | bytes 786440 | tf_op jit(solution)/shard_map/ppermute | solution.py:20
  41.6 12.3 %collective-permute-start.1 = (bf16[1,256,512]{2,1,0:T(8,128)(2,1)S(1)}, bf16[1,256,512]{2,1,0:T(8,128)(2,1)S(1)}, u32[]{:S(2)}, u32[]{:S(2)}) collective-permute-start(bf16[1,256,512]{2,1,0:T(8,128)(2,1)S(1)} %fusion.72), channel_id=1, source_target_pairs={{0,12},{4,16},{8,20},{12,24},{16,28},{1,13},{5,17},{9,21},{13,25},... | collective-permute-start | bytes 786440 | tf_op jit(solution)/shard_map/ppermute | solution.py:20
  45.9 12.9 %collective-permute-start.2 = (bf16[1,256,512]{2,1,0:T(8,128)(2,1)S(1)}, bf16[1,256,512]{2,1,0:T(8,128)(2,1)S(1)}, u32[]{:S(2)}, u32[]{:S(2)}) collective-permute-start(bf16[1,256,512]{2,1,0:T(8,128)(2,1)S(1)} %fusion.72), channel_id=1, source_target_pairs={{0,8},{4,12},{8,16},{12,20},{16,24},{20,28},{1,9},{5,13},{9,17},{1... | collective-permute-start | bytes 786440 | tf_op jit(solution)/shard_map/ppermute | solution.py:20
  47.3 11.6 %collective-permute-start.3 = (bf16[1,256,512]{2,1,0:T(8,128)(2,1)S(1)}, bf16[1,256,512]{2,1,0:T(8,128)(2,1)S(1)}, u32[]{:S(2)}, u32[]{:S(2)}) collective-permute-start(bf16[1,256,512]{2,1,0:T(8,128)(2,1)S(1)} %fusion.72), channel_id=1, source_target_pairs={{0,4},{4,8},{8,12},{12,16},{16,20},{20,24},{24,28},{1,5},{5,9},{9,... | collective-permute-start | bytes 786440 | tf_op jit(solution)/shard_map/ppermute | solution.py:20
  121.3 7.4 %slice-start = ((s8[5242880]{0:T(1024)(128)(4,1)}), s8[4194304]{0:T(1024)(128)(4,1)S(1)}, s32[]{:S(2)}) async-start(s8[5242880]{0:T(1024)(128)(4,1)} %bitcast.218), calls=%async_computation.7 | async-start | bytes 8388608 | tf_op jit(solution)/shard_map/while/body/eval_jaxpr/while
  125.2 2.0 copy-start.4
  125.3 3.4 slice-start.1
  128.7 4.2 copy-start.7
  132.9 2.8 copy-start.1
  132.9 2.8 copy-start.3
  145.3 7.4 %slice-start = ((s8[5242880]{0:T(1024)(128)(4,1)}), s8[4194304]{0:T(1024)(128)(4,1)S(1)}, s32[]{:S(2)}) async-start(s8[5242880]{0:T(1024)(128)(4,1)} %bitcast.218), calls=%async_computation.7 | async-start | bytes 8388608 | tf_op jit(solution)/shard_map/while/body/eval_jaxpr/while
  149.3 2.0 copy-start.4
  149.3 3.4 slice-start.1
  152.7 4.2 copy-start.7
  156.9 2.8 copy-start.1
  156.9 2.8 copy-start.3
  162.0 6.9 %copy-start.12 = (bf16[2,256,4,128]{1,3,2,0:T(8,128)(2,1)S(1)}, bf16[2,256,4,128]{1,3,2,0:T(8,128)(2,1)}, u32[]{:S(2)}) copy-start(bf16[2,256,4,128]{1,3,2,0:T(8,128)(2,1)} %get-tuple-element.82) | copy-start | bytes 1572868
  163.5 15.6 %collective-permute-start.4 = (bf16[1,256,512]{1,2,0:T(8,128)(2,1)S(1)}, bf16[1,256,512]{1,2,0:T(8,128)(2,1)S(1)}, u32[]{:S(2)}, u32[]{:S(2)}) collective-permute-start(bf16[1,256,512]{1,2,0:T(8,128)(2,1)S(1)} %get-tuple-element.154), channel_id=1, source_target_pairs={{4,0},{8,4},{12,8},{16,12},{20,16},{24,20},{28,24},{5,1},{9,5},{13... | collective-permute-start | bytes 786440 | tf_op jit(solution)/shard_map/ppermute | solution.py:20
  164.8 28.4 %collective-permute-start.7 = (bf16[1,256,512]{1,2,0:T(8,128)(2,1)S(1)}, bf16[1,256,512]{1,2,0:T(8,128)(2,1)S(1)}, u32[]{:S(2)}, u32[]{:S(2)}) collective-permute-start(bf16[1,256,512]{1,2,0:T(8,128)(2,1)S(1)} %get-tuple-element.155), channel_id=1, source_target_pairs={{16,0},{20,4},{24,8},{28,12},{17,1},{21,5},{25,9},{29,13},{18,2},{... | collective-permute-start | bytes 786440 | tf_op jit(solution)/shard_map/ppermute | solution.py:20
  166.1 27.1 %collective-permute-start.6 = (bf16[1,256,512]{1,2,0:T(8,128)(2,1)S(1)}, bf16[1,256,512]{1,2,0:T(8,128)(2,1)S(1)}, u32[]{:S(2)}, u32[]{:S(2)}) collective-permute-start(bf16[1,256,512]{1,2,0:T(8,128)(2,1)S(1)} %get-tuple-element.156), channel_id=1, source_target_pairs={{12,0},{16,4},{20,8},{24,12},{28,16},{13,1},{17,5},{21,9},{25,13},... | collective-permute-start | bytes 786440 | tf_op jit(solution)/shard_map/ppermute | solution.py:20
  167.4 25.8 %collective-permute-start.5 = (bf16[1,256,512]{1,2,0:T(8,128)(2,1)S(1)}, bf16[1,256,512]{1,2,0:T(8,128)(2,1)S(1)}, u32[]{:S(2)}, u32[]{:S(2)}) collective-permute-start(bf16[1,256,512]{1,2,0:T(8,128)(2,1)S(1)} %get-tuple-element.157), channel_id=1, source_target_pairs={{8,0},{12,4},{16,8},{20,12},{24,16},{28,20},{9,1},{13,5},{17,9},{2... | collective-permute-start | bytes 786440 | tf_op jit(solution)/shard_map/ppermute | solution.py:20
  209.0 213.8 %reduce-scatter.7.cloned.1.call-start = ((), (), s32[]{:S(2)}) async-start(), calls=%async_computation.6 | async-start | bytes 1638400
  397.0 3.8 copy-start.8
  397.0 3.9 copy-start.9
  397.0 4.0 copy-start.13
  401.1 2.3 copy-start.5
  (5 other events, 6.9 us)
Sparse Core Ops, SparseCore 0:
  9.6 25.2 all-gather.3
  36.5 34.4 all-gather.5
  72.5 34.4 all-gather.7
  209.2 185.3 reduce-scatter.4
  397.1 25.6 reduce-scatter.6
where the time goes:
time: 433 us; the launch traced here: 432 us
  waiting for transfers between devices  303 us (70%)
  matrix products  52.7 us (12%)
  other arithmetic  28.3 us (7%)
  starting transfers between devices  18.6 us (4%)
  local copies, waits for them, and re-layouts  15.2 us (4%)
  between operations  14.1 us (3%)
    reduce_scatter x1, waiting for transfers between devices, shards(): lax.psum_scatter(jnp.concatenate([term_in, term_out], axis=1).astype(jnp....  185 us
    all_gather x1, waiting for transfers between devices, shards(): lax.all_gather(w_out, 'fsdp', axis=0, tiled=True)  32.2 us
    ppermute x8, waiting for transfers between devices, from_behind(): lax.ppermute(value, axis, [(source, source + steps) for source in range(l...  31.4 us
    all_gather x1, waiting for transfers between devices, shards(): lax.all_gather(w_kv, 'fsdp', axis=0, tiled=True)  25.1 us
    unnamed x6, waiting for transfers between devices  18.7 us
    ppermute x8, starting transfers between devices, from_behind(): lax.ppermute(value, axis, [(source, source + steps) for source in range(l...  18.4 us
    concatenate x1, other arithmetic, shards(): jnp.concatenate([term_in, term_out], axis=1).astype(jnp.bfloat16)  12.7 us
    sub x2, matrix products, head_block(): expo = jnp.exp(scores - top)  10.4 us
  transfers between devices with their start and end apart: 13, of which 9 were waited for; matrix products, arithmetic and copies ran while one was open for 4% of the time, Pallas kernels for 0%

commit v1 on v0

--- a/solution.py
+++ b/solution.py
@@ -1,8 +1,11 @@
+import functools
 import math
 
 import jax
 import jax.numpy as jnp
 from jax import lax
+from jax.experimental import pallas as pl
+from jax.experimental.pallas import tpu as pltpu
 from jax.sharding import PartitionSpec as P
 
 QUERY_HEADS = 8
@@ -12,6 +15,275 @@
 
 
 EPS = 1e-05
+
+
+MESH = pl.DeviceIdType.MESH
+
+
+def gather_kernel(fsdp_count, q_in, kv_in, o_in, q_out, kv_out, o_out, own_sem, send_sem, recv_sem):
+    ctx_at = lax.axis_index("ctx")
+    fsdp_at = lax.axis_index("fsdp")
+    half_at = lax.rem(ctx_at, 2)
+    side = ctx_at + 1 - 2 * half_at
+    core = fsdp_at + 1 - 2 * lax.rem(fsdp_at, 2)
+    across = lax.rem(fsdp_at + fsdp_count // 2, fsdp_count)
+    across_core = lax.rem(core + fsdp_count // 2, fsdp_count)
+    ins, outs = ((q_in, kv_in, o_in), (q_out, kv_out, o_out))
+    rows = q_in.shape[0]
+    half = rows // 2
+    pieces = []
+    for index in (1, 0, 2):
+        cuts = 1 if index == 1 else 2
+        for cut in range(cuts):
+            pieces.append((index, cut * (half // cuts), half // cuts))
+    count = len(pieces)
+
+    barrier = pltpu.get_barrier_semaphore()
+    for target in ((ctx_at, core), (ctx_at, across), (side, fsdp_at)):
+        pl.semaphore_signal(barrier, inc=1, device_id=target, device_id_type=MESH)
+    pl.semaphore_wait(barrier, 3)
+
+    def at(ref, owner, which, piece):
+        _, start, size = piece
+        return ref.at[pl.ds(pl.multiple_of(owner * rows + which * half + start, 128), size)]
+
+    def remote(src, dst, slot, target):
+        return pltpu.make_async_remote_copy(
+            src_ref=src, dst_ref=dst, send_sem=send_sem.at[slot], recv_sem=recv_sem.at[slot],
+            device_id=target, device_id_type=MESH,
+        )
+
+    y_copies = []
+    for i, piece in enumerate(pieces):
+        index, start, size = piece
+        copy = remote(
+            ins[index].at[pl.ds(pl.multiple_of(half_at * half + start, 128), size)],
+            at(outs[index], fsdp_at, half_at, piece), i, (ctx_at, across),
+        )
+        copy.start()
+        y_copies.append(copy)
+    own_copies, core_copies = ([], [])
+    for index in (1, 0, 2):
+        place = outs[index].at[pl.ds(pl.multiple_of(fsdp_at * rows, 128), rows)]
+        copy = remote(ins[index], place, 4 * count + index, (ctx_at, core))
+        copy.start()
+        core_copies.append(copy)
+        copy = pltpu.make_async_copy(ins[index], place, own_sem.at[index])
+        copy.start()
+        own_copies.append(copy)
+    x_copies = []
+    for i, piece in enumerate(pieces):
+        out = outs[piece[0]]
+        here = at(out, across, half_at, piece)
+        remote(here, here, i, (ctx_at, across)).wait_recv()
+        copy = remote(here, here, count + i, (side, fsdp_at))
+        copy.start()
+        x_copies.append(copy)
+        copy = remote(here, here, 2 * count + i, (ctx_at, core))
+        copy.start()
+        core_copies.append(copy)
+    for i, piece in enumerate(pieces):
+        here = at(outs[piece[0]], across, 1 - half_at, piece)
+        remote(here, here, count + i, (side, fsdp_at)).wait_recv()
+        copy = remote(here, here, 3 * count + i, (ctx_at, core))
+        copy.start()
+        core_copies.append(copy)
+    for i, piece in enumerate(pieces):
+        for level, which in ((2, half_at), (3, 1 - half_at)):
+            here = at(outs[piece[0]], across_core, which, piece)
+            remote(here, here, level * count + i, (ctx_at, core)).wait_recv()
+    for index in range(3):
+        place = outs[index].at[pl.ds(pl.multiple_of(core * rows, 128), rows)]
+        remote(ins[index], place, 4 * count + index, (ctx_at, core)).wait_recv()
+    for copy in y_copies + x_copies + core_copies:
+        copy.wait_send()
+    for copy in own_copies:
+        copy.wait()
+
+
+def gather_weights(w_q, w_kv, w_out):
+    count = lax.axis_size("fsdp")
+    shapes = [
+        jax.ShapeDtypeStruct((count * w.shape[0], w.shape[1]), w.dtype) for w in (w_q, w_kv, w_out)
+    ]
+    slots = 4 * 5 + 3
+    return pl.pallas_call(
+        functools.partial(gather_kernel, count),
+        out_shape=shapes,
+        in_specs=[pl.BlockSpec(memory_space=pl.ANY)] * 3,
+        out_specs=[pl.BlockSpec(memory_space=pl.ANY)] * 3,
+        scratch_shapes=[
+            pltpu.SemaphoreType.DMA((3,)),
+            pltpu.SemaphoreType.DMA((slots,)),
+            pltpu.SemaphoreType.DMA((slots,)),
+        ],
+        compiler_params=pltpu.CompilerParams(collective_id=0, has_side_effects=True),
+        name="gather_weights",
+    )(w_q, w_kv, w_out)
+
+
+def reduce_plan(ctx_count, fsdp_count):
+    ctx_bits = [("ctx", 1 << i) for i in range(ctx_count.bit_length() - 1)]
+    fsdp_bits = [("fsdp", 1 << i) for i in range(fsdp_count.bit_length() - 1)]
+    core, rest = (fsdp_bits[0], fsdp_bits[1:])
+    order_a = rest + ctx_bits
+    order_b = ctx_bits + rest
+    order_c = ctx_bits[1:2] + rest + ctx_bits[:1] + ctx_bits[2:]
+    return core, order_a, order_b, order_c
+
+
+def reduce_parts(widths):
+    q_width, kv_width, o_width = widths
+    tail = 128
+    return (
+        (0, 0, q_width - tail, 0),
+        (2, 0, o_width - tail, 1),
+        (1, 0, kv_width, 2),
+        (0, q_width - tail, tail, 2),
+        (2, o_width - tail, tail, 2),
+    )
+
+
+def reduce_kernel(ctx_count, fsdp_count, parts, scale, *refs):
+    terms, out_ref, refs = (refs[:3], refs[3], refs[4:])
+    core, *orders = reduce_plan(ctx_count, fsdp_count)
+    stages = len(orders[0])
+    accs, recvs = ([], [])
+    for _ in parts:
+        accs.append(refs[: stages])
+        recvs.append(refs[stages : 2 * stages + 1])
+        refs = refs[2 * stages + 1 :]
+    own_sem, send_sem, recv_sem = refs
+    place = {"ctx": lax.axis_index("ctx"), "fsdp": lax.axis_index("fsdp")}
+    count = ctx_count * fsdp_count
+    block = terms[0].shape[0] // count
+    offsets = (0, terms[0].shape[1], terms[0].shape[1] + terms[1].shape[1])
+
+    def my_bit(bit):
+        return lax.rem(place[bit[0]] // bit[1], 2)
+
+    def partner(bit):
+        flipped = place[bit[0]] + bit[1] * (1 - 2 * my_bit(bit))
+        return (flipped, place["fsdp"]) if bit[0] == "ctx" else (place["ctx"], flipped)
+
+    barrier = pltpu.get_barrier_semaphore()
+    for bit in [core] + orders[0]:
+        pl.semaphore_signal(barrier, inc=1, device_id=partner(bit), device_id_type=MESH)
+    pl.semaphore_wait(barrier, stages + 1)
+
+    half_blocks = count // 2
+    for p, (index, start, width, order) in enumerate(parts):
+        columns = pl.ds(start, width)
+
+        def one(j, carry):
+            owner = 0
+            for i, bit in enumerate(orders[order]):
+                digit = lax.rem(j // (half_blocks >> (i + 1)), 2)
+                owner = owner + digit * bit[1] * (fsdp_count if bit[0] == "ctx" else 1)
+            slot = pl.ds(pl.multiple_of(j * block, block), block)
+
+            def rows(core_bit):
+                return pl.ds(pl.multiple_of((owner + core_bit * core[1]) * block, block), block)
+
+            pltpu.make_async_remote_copy(
+                src_ref=terms[index].at[rows(1 - my_bit(core)), columns],
+                dst_ref=recvs[p][0].at[slot],
+                send_sem=send_sem.at[p, 0], recv_sem=recv_sem.at[p, 0],
+                device_id=partner(core), device_id_type=MESH,
+            ).start()
+            pltpu.make_async_copy(
+                terms[index].at[rows(my_bit(core)), columns], accs[p][0].at[slot], own_sem.at[p]
+            ).start()
+            return carry
+
+        lax.fori_loop(0, half_blocks, one, 0)
+
+    def add(target, first, base, second, size, last):
+        step = min(size, 64)
+
+        def body(i, carry):
+            at = pl.multiple_of(i * step, step)
+            value = first[pl.ds(pl.multiple_of(base + at, step), step)].astype(jnp.float32)
+            value = value + second[pl.ds(at, step)].astype(jnp.float32)
+            if last is None:
+                target[pl.ds(at, step)] = value.astype(target.dtype)
+            else:
+                target[pl.ds(at, step), last] = value * scale
+            return carry
+
+        lax.fori_loop(0, size // step, body, 0)
+
+    half_rows = half_blocks * block
+    sends, latest = ([], {})
+    for stage in range(stages + 1):
+        size = half_rows >> stage
+        for p, (index, start, width, order) in enumerate(parts):
+            if stage == 0:
+                whole = terms[index].at[pl.ds(0, half_rows), pl.ds(start, width)]
+                pltpu.make_async_copy(whole, accs[p][0], own_sem.at[p]).wait()
+                copy = pltpu.make_async_remote_copy(
+                    src_ref=whole, dst_ref=recvs[p][0],
+                    send_sem=send_sem.at[p, 0], recv_sem=recv_sem.at[p, 0],
+                    device_id=partner(core), device_id_type=MESH,
+                )
+                copy.wait_recv()
+                sends.append(copy)
+                target, base, source = (accs[p][0], 0, accs[p][0])
+            else:
+                bit = orders[order][stage - 1]
+                latest[p].wait_recv()
+                source = accs[p][stage - 1]
+                base = my_bit(bit) * size
+                target = accs[p][stage] if stage < stages else out_ref
+            last = pl.ds(offsets[index] + start, width) if stage == stages else None
+            add(target, source, base, recvs[p][stage], size, last)
+            if stage < stages:
+                bit = orders[order][stage]
+                send_from = pl.multiple_of((1 - my_bit(bit)) * (size // 2), size // 2)
+                copy = pltpu.make_async_remote_copy(
+                    src_ref=target.at[pl.ds(send_from, size // 2)],
+                    dst_ref=recvs[p][stage + 1],
+                    send_sem=send_sem.at[p, stage + 1], recv_sem=recv_sem.at[p, stage + 1],
+                    device_id=partner(bit), device_id_type=MESH,
+                )
+                copy.start()
+                latest[p] = copy
+                sends.append(copy)
+    for copy in sends:
+        copy.wait_send()
+
+
+def reduce_terms(term_q, term_kv, term_o, scale):
+    ctx_count, fsdp_count = (lax.axis_size("ctx"), lax.axis_size("fsdp"))
+    terms = (term_q, term_kv, term_o)
+    widths = [t.shape[1] for t in terms]
+    parts = reduce_parts(widths)
+    count = ctx_count * fsdp_count
+    block = term_q.shape[0] // count
+    stages = count.bit_length() - 2
+    scratch = []
+    for _, _, width, _ in parts:
+        half_rows = count // 2 * block
+        for stage in range(stages):
+            scratch.append(pltpu.VMEM((half_rows >> stage, width), jnp.bfloat16))
+        for stage in range(stages + 1):
+            scratch.append(pltpu.VMEM((half_rows >> stage, width), jnp.bfloat16))
+    scratch += [
+        pltpu.SemaphoreType.DMA((len(parts),)),
+        pltpu.SemaphoreType.DMA((len(parts), stages + 1)),
+        pltpu.SemaphoreType.DMA((len(parts), stages + 1)),
+    ]
+    return pl.pallas_call(
+        functools.partial(reduce_kernel, ctx_count, fsdp_count, parts, scale),
+        out_shape=jax.ShapeDtypeStruct((block, sum(widths)), jnp.float32),
+        in_specs=[pl.BlockSpec(memory_space=pl.ANY)] * 3,
+        out_specs=pl.BlockSpec(memory_space=pltpu.VMEM),
+        scratch_shapes=scratch,
+        compiler_params=pltpu.CompilerParams(
+            collective_id=1, has_side_effects=True, vmem_limit_bytes=40 * 1024 * 1024
+        ),
+        name="reduce_terms",
+    )(*terms)
 
 
 def from_behind(value, axis, steps):
@@ -94,11 +366,7 @@
 
 
 def shards(x_cur, x_next, cot_cur, cot_next, w_q, w_kv, w_out):
-    full_q, full_kv, full_out = (
-        lax.all_gather(w_q, "fsdp", axis=0, tiled=True),
-        lax.all_gather(w_kv, "fsdp", axis=0, tiled=True),
-        lax.all_gather(w_out, "fsdp", axis=0, tiled=True),
-    )
+    full_q, full_kv, full_out = gather_weights(w_q, w_kv, w_out)
     seq_count, shard, width = x_cur.shape
     base = lax.axis_index("ctx") * shard
     preds = WINDOW_TOKENS // shard
@@ -144,28 +412,26 @@
     grad_cur = (cot_cur.astype(jnp.float32) + grad_x).astype(jnp.bfloat16)
     hidden_rows = hidden.reshape(seq_count * shard, width)
     cot_rows = cot_next.reshape(seq_count * shard, width)
-    left_rows = jnp.concatenate([grad_query, grad_kv], axis=2).reshape(seq_count * shard, -1)
+    query_left = grad_query.reshape(seq_count * shard, -1)
+    keyval_left = grad_kv.reshape(seq_count * shard, -1)
     attended_rows = attended.reshape(seq_count * shard, -1)
     contract_rows = (((0,), (0,)), ((), ()))
     ctx_count = lax.axis_size("ctx")
     fsdp_count = lax.axis_size("fsdp")
-    term_in = lax.dot_general(
-        hidden_rows, left_rows, contract_rows, preferred_element_type=jnp.float32
+    term_q, term_kv = (
+        lax.dot_general(hidden_rows, left, contract_rows, preferred_element_type=jnp.float32)
+        for left in (query_left, keyval_left)
     )
     term_out = 2.0 * lax.dot_general(
         cot_rows, attended_rows, contract_rows, preferred_element_type=jnp.float32
     )
-    summed = lax.psum_scatter(
-        jnp.concatenate([term_in, term_out], axis=1).astype(jnp.bfloat16),
-        "ctx",
-        scatter_dimension=0,
-        tiled=True,
-    ).astype(jnp.float32)
-    summed = lax.psum_scatter(
-        summed.astype(jnp.bfloat16), "fsdp", scatter_dimension=0, tiled=True
-    ).astype(jnp.float32)
     token_total = seq_count * shard * ctx_count * fsdp_count
-    grad_weights = summed * (1.0 / math.sqrt(token_total))
+    grad_weights = reduce_terms(
+        term_q.astype(jnp.bfloat16),
+        term_kv.astype(jnp.bfloat16),
+        term_out.astype(jnp.bfloat16),
+        1.0 / math.sqrt(token_total),
+    )
     return (x_prev, grad_cur, grad_weights)
 
 

time: 433 us -> 290 us (0.67)
  waiting for transfers between devices: 303 us -> 29.9 us
  Pallas kernels: 0 us -> 154 us
  between operations: 14.1 us -> 1 us
  other arithmetic: 28.3 us -> 15.5 us
    reduce_scatter x1 -> x0, waiting for transfers between devices: 185 us -> none  [shards(): lax.psum_scatter(jnp.concatenate([term_in, term_out], axis=1).astype(jnp....]
    pallas_call x0 -> x2, Pallas kernels: none -> 154 us  [the longest x1 84 us: gather_weights(): pl.pallas_call(functools.partial(gather_kernel, count), out_shape=shapes,...]
    all_gather x3 -> x0, waiting for transfers between devices: 67.3 us -> none  [the longest x1 32.2 us: shards(): lax.all_gather(w_out, 'fsdp', axis=0, tiled=True)]
    unnamed x6 -> x0, waiting for transfers between devices: 18.7 us -> none
    concatenate x1 -> x0, other arithmetic: 12.7 us -> none  [shards(): jnp.concatenate([term_in, term_out], axis=1).astype(jnp.bfloat16)]
  transfers between devices with their start and end apart: 13 -> 8, of which waited for: 9 -> 1; matrix products, arithmetic and copies ran while one was open for 4% -> 6% of each run, Pallas kernels for 0% -> 0%
where the time goes in v1:
time: 290 us; the launch traced here: 289 us
  Pallas kernels  154 us (53%)
  matrix products  53.1 us (18%)
  waiting for transfers between devices  29.9 us (10%)
  starting transfers between devices  19.7 us (7%)
  local copies, waits for them, and re-layouts  15.5 us (5%)
  other arithmetic  15.5 us (5%)
    pallas_call x1, Pallas kernels, gather_weights(): pl.pallas_call(functools.partial(gather_kernel, count), out_shape=shapes,...  84 us
    pallas_call x1, Pallas kernels, reduce_terms(): pl.pallas_call(functools.partial(reduce_kernel, ctx_count, fsdp_count, pa...  69.6 us
    ppermute x8, waiting for transfers between devices, from_behind(): lax.ppermute(value, axis, [(source, source + steps) for source in range(l...  29.9 us
    ppermute x8, starting transfers between devices, from_behind(): lax.ppermute(value, axis, [(source, source + steps) for source in range(l...  19.7 us
    sub x2, matrix products, head_block(): expo = jnp.exp(scores - top)  10.4 us
    dot_general x2, matrix products, head_block(): jnp.einsum('imd,jd->mij', grad3, vals2, preferred_element_type=jnp.float32)  7.96 us
    convert_element_type x2, other arithmetic, head_block(): probs_low = probs.astype(jnp.bfloat16)  7.95 us
  transfers between devices with their start and end apart: 8, of which 1 were waited for; matrix products, arithmetic and copies ran while one was open for 6% of the time, Pallas kernels for 0%

profile of v1, /device:TPU:0, one launch (start us, length us, event | category | flops | bytes accessed | tf_op | source)
XLA Modules:
  0.0 288.6 jit_solution(11200350514806180240)
XLA Ops:
  0.7 1.7 fusion.70
  2.3 84.0 %gather_weights.1 = (bf16[2048,1024]{1,0:T(8,128)(2,1)}, bf16[2048,512]{1,0:T(8,128)(2,1)}, bf16[2048,1024]{1,0:T(8,128)(2,1)}) custom-call(bf16[512,1024]{1,0:T(8,128)(2,1)} %q_in.1, bf16[512,512]{1,0:T(8,128)(2,1)} %kv_in.1, bf16[512,1024]{1,0:T(8,128)(2,1)} %o_in.1), custom_call_target="tpu_custom_call" | custom-call | tf_op jit(solution)/shard_map/gather_weights/pallas_call | solution.py:110
  86.3 2.3 fusion.72
  88.6 4.1 %collective-permute-start.3 = (bf16[1,256,512]{2,1,0:T(8,128)(2,1)S(1)}, bf16[1,256,512]{2,1,0:T(8,128)(2,1)}, u32[]{:S(2)}, u32[]{:S(2)}) collective-permute-start(bf16[1,256,512]{2,1,0:T(8,128)(2,1)S(1)} %fusion.72), channel_id=1, source_target_pairs={{0,4},{4,8},{8,12},{12,16},{16,20},{20,24},{24,28},{1,5},{5,9},{9,... | collective-permute-start | bytes 786440 | tf_op jit(solution)/shard_map/ppermute | solution.py:292
  92.7 3.5 %collective-permute-start.2 = (bf16[1,256,512]{2,1,0:T(8,128)(2,1)S(1)}, bf16[1,256,512]{2,1,0:T(8,128)(2,1)}, u32[]{:S(2)}, u32[]{:S(2)}) collective-permute-start(bf16[1,256,512]{2,1,0:T(8,128)(2,1)S(1)} %fusion.72), channel_id=1, source_target_pairs={{0,8},{4,12},{8,16},{12,20},{16,24},{20,28},{1,9},{5,13},{9,17},{1... | collective-permute-start | bytes 786440 | tf_op jit(solution)/shard_map/ppermute | solution.py:292
  96.2 4.5 %collective-permute-start.1 = (bf16[1,256,512]{2,1,0:T(8,128)(2,1)S(1)}, bf16[1,256,512]{2,1,0:T(8,128)(2,1)}, u32[]{:S(2)}, u32[]{:S(2)}) collective-permute-start(bf16[1,256,512]{2,1,0:T(8,128)(2,1)S(1)} %fusion.72), channel_id=1, source_target_pairs={{0,12},{4,16},{8,20},{12,24},{16,28},{1,13},{5,17},{9,21},{13,25},... | collective-permute-start | bytes 786440 | tf_op jit(solution)/shard_map/ppermute | solution.py:292
  100.7 2.0 collective-permute-start
  102.7 3.5 %convolution_convert_fusion.3 = bf16[256,1024]{1,0:T(8,128)(2,1)S(1)} fusion(bf16[2048,1024]{1,0:T(8,128)(2,1)} %get-tuple-element.86, bf16[1,256,2048]{2,1,0:T(8,128)(2,1)S(1)} %copy-done.2, f32[256]{0:T(256)S(1)} %add_rsqrt_fusion), kind=kOutput, calls=%fused_computation.87 | convolution fusion | flops 1075576832 | bytes 5768192 | tf_op jit(solution)/shard_map/sid,dc->sic/dot_general | solution.py:375
  106.2 4.3 %fusion.71 = bf16[1024,256]{1,0:T(8,128)(2,1)} fusion(bf16[2048,1024]{1,0:T(8,128)(2,1)} %get-tuple-element.87, bf16[1,256,2048]{2,1,0:T(8,128)(2,1)S(1)} %copy-done), kind=kOutput, calls=%fused_computation.86 | convolution fusion | flops 1074266112 | bytes 5767168 | tf_op jit(solution)/shard_map/sid,dc->sic/dot_general | solution.py:382
  111.8 2.1 copy.26
  119.9 48.1 %while.29 = (s32[]{:T(128)}, bf16[2,256,4,128]{1,3,2,0:T(8,128)(2,1)}, bf16[2,256,4,128]{1,3,2,0:T(8,128)(2,1)}, bf16[2,1280,128]{1,2,0:T(8,128)(2,1)}, bf16[2,1...) while((s32[]{:T(128)}, ...), condition=%wide.region_4.5_spmd.clone, body=%wide.region_1.4_spmd.clone.sunk | while | flops 2030305536 | bytes 79461984 | solution.py:353
  122.1 5.2 %exponential_reduce_fusion.2 = (f32[4,256]{1,0:T(4,128)S(1)}, f32[4,256,1280]{1,2,0:T(8,128)}) fusion(pred[256,1280]{0,1:T(8,128)(4,1)S(1)} %fusion.133, bf16[2,1280,128]{2,1,0:T(8,128)(2,1)} %get-tuple-element.276, s32[]{:T(128)S(6)} %copy.72, bf16[2,256,4,128]{3,1,2,0:T(8,128)(2,1)} %get-tuple-element.277), kind=kOutput, calls=%fused_computation.9.clone.1 | convolution fusion | flops 340788480 | bytes 6165504 | tf_op jit(solution)/shard_map/while/body/eval_jaxpr/while/body/eval_jaxpr/sub | solution.py:307
  127.3 4.0 %fusion.134 = bf16[4,256,1280]{1,2,0:T(8,128)(2,1)S(1)} fusion(f32[4,256]{1,0:T(4,128)S(1)} %get-tuple-element.238, f32[4,256,1280]{1,2,0:T(8,128)} %get-tuple-element.239), kind=kLoop, calls=%fused_computation.18.clone.1 | loop fusion | flops 2621440 | bytes 7868416 | tf_op jit(solution)/shard_map/while/body/eval_jaxpr/while/body/eval_jaxpr/convert_element_type | solution.py:309
  131.3 1.9 fusion.139
  134.7 4.0 %fusion.137 = bf16[4,256,1280]{1,2,0:T(8,128)(2,1)} fusion(f32[4,256]{1,0:T(4,128)S(1)} %fusion.136, f32[4,256]{1,0:T(4,128)S(1)} %get-tuple-element.238, f32[4,256,1280]{1,2,0:T(8,128)S(1)} %bitcast.217, bf16[2,1280,128]{1,2,0:T(8,128)(2,1)S(1)} %copy-done.4, s32[]{:T(128)S(6)} %copy.72, bf16[2,256,4,128]{3,1,2,0:T(8,128)(2,1)} %get-tuple-element.278), kind=kOutput, calls=%fused_computation.6.clone.1 | convolution fusion | flops 342097920 | bytes 8463360 | tf_op jit(solution)/shard_map/while/body/eval_jaxpr/while/body/eval_jaxpr/imd,jd->mij/dot_general | solution.py:311
  138.9 2.7 fusion.140
  146.1 5.2 %exponential_reduce_fusion.2 = (f32[4,256]{1,0:T(4,128)S(1)}, f32[4,256,1280]{1,2,0:T(8,128)}) fusion(pred[256,1280]{0,1:T(8,128)(4,1)S(1)} %fusion.133, bf16[2,1280,128]{2,1,0:T(8,128)(2,1)} %get-tuple-element.276, s32[]{:T(128)S(6)} %copy.72, bf16[2,256,4,128]{3,1,2,0:T(8,128)(2,1)} %get-tuple-element.277), kind=kOutput, calls=%fused_computation.9.clone.1 | convolution fusion | flops 340788480 | bytes 6165504 | tf_op jit(solution)/shard_map/while/body/eval_jaxpr/while/body/eval_jaxpr/sub | solution.py:307
  151.3 4.0 %fusion.134 = bf16[4,256,1280]{1,2,0:T(8,128)(2,1)S(1)} fusion(f32[4,256]{1,0:T(4,128)S(1)} %get-tuple-element.238, f32[4,256,1280]{1,2,0:T(8,128)} %get-tuple-element.239), kind=kLoop, calls=%fused_computation.18.clone.1 | loop fusion | flops 2621440 | bytes 7868416 | tf_op jit(solution)/shard_map/while/body/eval_jaxpr/while/body/eval_jaxpr/convert_element_type | solution.py:309
  155.3 1.9 fusion.139
  158.8 4.0 %fusion.137 = bf16[4,256,1280]{1,2,0:T(8,128)(2,1)} fusion(f32[4,256]{1,0:T(4,128)S(1)} %fusion.136, f32[4,256]{1,0:T(4,128)S(1)} %get-tuple-element.238, f32[4,256,1280]{1,2,0:T(8,128)S(1)} %bitcast.217, bf16[2,1280,128]{1,2,0:T(8,128)(2,1)S(1)} %copy-done.4, s32[]{:T(128)S(6)} %copy.72, bf16[2,256,4,128]{3,1,2,0:T(8,128)(2,1)} %get-tuple-element.278), kind=kOutput, calls=%fused_computation.6.clone.1 | convolution fusion | flops 342097920 | bytes 8463360 | tf_op jit(solution)/shard_map/while/body/eval_jaxpr/while/body/eval_jaxpr/imd,jd->mij/dot_general | solution.py:311
  163.0 2.7 fusion.140
  168.1 3.7 %fusion.86 = f32[256,2048]{1,0:T(8,128)S(1)} fusion(bf16[256,1024]{0,1:T(8,128)(2,1)} %bitcast.17, bf16[2048,1024]{1,0:T(8,128)(2,1)} %get-tuple-element.86), kind=kOutput, calls=%fused_computation.109 | convolution fusion | flops 1073741824 | bytes 6815744 | tf_op jit(solution)/shard_map/sic,dc->sid/dot_general | solution.py:405
  171.8 2.6 convolution_convert_fusion.1.refs_0_
  174.6 1.6 collective-permute-start.4
  176.2 1.3 collective-permute-start.7
  177.5 1.3 collective-permute-start.6
  178.8 1.5 collective-permute-start.5
  180.3 2.3 fusion.64
  182.6 1.3 fusion.57.refs_2_
  183.9 29.9 %collective-permute-done.7 = bf16[1,256,512]{1,2,0:T(8,128)(2,1)S(1)} collective-permute-done((bf16[1,256,512]{1,2,0:T(8,128)(2,1)S(1)}, bf16[1,256,512]{1,2,0:T(8,128)(2,1)S(1)}, u32[]{:S(2)}, u32[]{:S(2)}) %collective-permute-start.7) | collective-permute-done | bytes 262176 | tf_op jit(solution)/shard_map/ppermute | solution.py:292
  216.6 69.6 %reduce_terms.1 = f32[64,2560]{1,0:T(8,128)S(1)} custom-call(bf16[2048,1024]{1,0:T(8,128)(2,1)S(1)} %convolution_convert_fusion.1.refs_0_, bf16[2048,512]{1,0:T(8,128)(2,1)S(1)} %convolution_convert_fusion.2.refs_1_, bf16[2048,1024]{1,0:T(8,128)(2,1)S(1)} %fusion.57.refs_2_), custom_call_target="tpu_custom_call" | custom-call | tf_op jit(solution)/shard_map/reduce_terms/pallas_call | solution.py:276
  286.2 1.6 fusion.69
  (102 shorter events, 23.3 us)
Async XLA Ops:
  0.6 105.6 %copy-start = (bf16[1,256,2048]{2,1,0:T(8,128)(2,1)S(1)}, bf16[1,256,2048]{2,1,0:T(8,128)(2,1)}, u32[]{:S(2)}) copy-start(bf16[1,256,2048]{2,1,0:T(8,128)(2,1)} %param.12) | copy-start | bytes 3145732
  0.6 85.7 %copy-start.2 = (bf16[1,256,2048]{2,1,0:T(8,128)(2,1)S(1)}, bf16[1,256,2048]{2,1,0:T(8,128)(2,1)}, u32[]{:S(2)}) copy-start(bf16[1,256,2048]{2,1,0:T(8,128)(2,1)} %param.9) | copy-start | bytes 3145732
  88.6 28.2 %collective-permute-start.3 = (bf16[1,256,512]{2,1,0:T(8,128)(2,1)S(1)}, bf16[1,256,512]{2,1,0:T(8,128)(2,1)}, u32[]{:S(2)}, u32[]{:S(2)}) collective-permute-start(bf16[1,256,512]{2,1,0:T(8,128)(2,1)S(1)} %fusion.72), channel_id=1, source_target_pairs={{0,4},{4,8},{8,12},{12,16},{16,20},{20,24},{24,28},{1,5},{5,9},{9,... | collective-permute-start | bytes 786440 | tf_op jit(solution)/shard_map/ppermute | solution.py:292
  92.7 23.1 %collective-permute-start.2 = (bf16[1,256,512]{2,1,0:T(8,128)(2,1)S(1)}, bf16[1,256,512]{2,1,0:T(8,128)(2,1)}, u32[]{:S(2)}, u32[]{:S(2)}) collective-permute-start(bf16[1,256,512]{2,1,0:T(8,128)(2,1)S(1)} %fusion.72), channel_id=1, source_target_pairs={{0,8},{4,12},{8,16},{12,20},{16,24},{20,28},{1,9},{5,13},{9,17},{1... | collective-permute-start | bytes 786440 | tf_op jit(solution)/shard_map/ppermute | solution.py:292
  96.2 18.6 %collective-permute-start.1 = (bf16[1,256,512]{2,1,0:T(8,128)(2,1)S(1)}, bf16[1,256,512]{2,1,0:T(8,128)(2,1)}, u32[]{:S(2)}, u32[]{:S(2)}) collective-permute-start(bf16[1,256,512]{2,1,0:T(8,128)(2,1)S(1)} %fusion.72), channel_id=1, source_target_pairs={{0,12},{4,16},{8,20},{12,24},{16,28},{1,13},{5,17},{9,21},{13,25},... | collective-permute-start | bytes 786440 | tf_op jit(solution)/shard_map/ppermute | solution.py:292
  100.7 13.1 %collective-permute-start = (bf16[1,256,512]{2,1,0:T(8,128)(2,1)S(1)}, bf16[1,256,512]{2,1,0:T(8,128)(2,1)}, u32[]{:S(2)}, u32[]{:S(2)}) collective-permute-start(bf16[1,256,512]{2,1,0:T(8,128)(2,1)S(1)} %fusion.72), channel_id=1, source_target_pairs={{0,16},{4,20},{8,24},{12,28},{1,17},{5,21},{9,25},{13,29},{2,18},{... | collective-permute-start | bytes 786440 | tf_op jit(solution)/shard_map/ppermute | solution.py:292
  127.3 7.4 %slice-start = ((s8[5242880]{0:T(1024)(128)(4,1)}), s8[4194304]{0:T(1024)(128)(4,1)S(1)}, s32[]{:S(2)}) async-start(s8[5242880]{0:T(1024)(128)(4,1)} %bitcast.216), calls=%async_computation | async-start | bytes 8388608 | tf_op jit(solution)/shard_map/while/body/eval_jaxpr/while
  131.3 2.0 copy-start.4
  131.3 2.0 copy-start.12
  131.3 3.4 %slice-start.1 = ((s8[5242880]{0:T(1024)(128)(4,1)}), s8[1048576]{0:T(1024)(128)(4,1)S(1)}, s32[]{:S(2)}) async-start(s8[5242880]{0:T(1024)(128)(4,1)} %bitcast.216), calls=%async_computation.1 | async-start | bytes 2097152 | tf_op jit(solution)/shard_map/while/body/eval_jaxpr/while
  133.8 0.8 copy-start.13
  134.7 4.2 %copy-start.9 = (bf16[2,256,4,128]{3,1,2,0:T(8,128)(2,1)S(1)}, bf16[2,256,4,128]{3,1,2,0:T(8,128)(2,1)}, u32[]{:S(2)}) copy-start(bf16[2,256,4,128]{3,1,2,0:T(8,128)(2,1)} %get-tuple-element.277) | copy-start | bytes 1572868 | tf_op jit(solution)/shard_map/while/body/eval_jaxpr/while
  138.9 2.8 copy-start.1
  138.9 2.8 copy-start.3
  151.3 7.4 %slice-start = ((s8[5242880]{0:T(1024)(128)(4,1)}), s8[4194304]{0:T(1024)(128)(4,1)S(1)}, s32[]{:S(2)}) async-start(s8[5242880]{0:T(1024)(128)(4,1)} %bitcast.216), calls=%async_computation | async-start | bytes 8388608 | tf_op jit(solution)/shard_map/while/body/eval_jaxpr/while
  155.3 2.0 copy-start.4
  155.3 2.0 copy-start.12
  155.3 3.4 %slice-start.1 = ((s8[5242880]{0:T(1024)(128)(4,1)}), s8[1048576]{0:T(1024)(128)(4,1)S(1)}, s32[]{:S(2)}) async-start(s8[5242880]{0:T(1024)(128)(4,1)} %bitcast.216), calls=%async_computation.1 | async-start | bytes 2097152 | tf_op jit(solution)/shard_map/while/body/eval_jaxpr/while
  158.8 4.2 %copy-start.9 = (bf16[2,256,4,128]{3,1,2,0:T(8,128)(2,1)S(1)}, bf16[2,256,4,128]{3,1,2,0:T(8,128)(2,1)}, u32[]{:S(2)}) copy-start(bf16[2,256,4,128]{3,1,2,0:T(8,128)(2,1)} %get-tuple-element.277) | copy-start | bytes 1572868 | tf_op jit(solution)/shard_map/while/body/eval_jaxpr/while
  162.9 2.8 copy-start.1
  163.0 2.8 copy-start.3
  171.7 2.7 copy-start.7
  171.7 2.7 copy-start.8
  171.8 8.5 %copy-start.11 = (bf16[1,256,2048]{2,1,0:T(8,128)(2,1)S(1)}, bf16[1,256,2048]{2,1,0:T(8,128)(2,1)}, u32[]{:S(2)}) copy-start(bf16[1,256,2048]{2,1,0:T(8,128)(2,1)} %param.10) | copy-start | bytes 3145732
  174.4 5.9 %copy-start.10 = (bf16[2048,1024]{1,0:T(8,128)(2,1)S(1)}, bf16[2048,1024]{1,0:T(8,128)(2,1)}, u32[]{:S(2)}) copy-start(bf16[2048,1024]{1,0:T(8,128)(2,1)} %get-tuple-element.87) | copy-start | bytes 12582916
  174.4 5.9 %copy-start.14 = (bf16[2,256,4,128]{1,3,2,0:T(8,128)(2,1)S(1)}, bf16[2,256,4,128]{1,3,2,0:T(8,128)(2,1)}, u32[]{:S(2)}) copy-start(bf16[2,256,4,128]{1,3,2,0:T(8,128)(2,1)} %get-tuple-element.88) | copy-start | bytes 1572868
  174.6 9.3 %collective-permute-start.4 = (bf16[1,256,512]{1,2,0:T(8,128)(2,1)S(1)}, bf16[1,256,512]{1,2,0:T(8,128)(2,1)S(1)}, u32[]{:S(2)}, u32[]{:S(2)}) collective-permute-start(bf16[1,256,512]{1,2,0:T(8,128)(2,1)S(1)} %get-tuple-element.151), channel_id=1, source_target_pairs={{4,0},{8,4},{12,8},{16,12},{20,16},{24,20},{28,24},{5,1},{9,5},{13... | collective-permute-start | bytes 786440 | tf_op jit(solution)/shard_map/ppermute | solution.py:292
  176.2 37.7 %collective-permute-start.7 = (bf16[1,256,512]{1,2,0:T(8,128)(2,1)S(1)}, bf16[1,256,512]{1,2,0:T(8,128)(2,1)S(1)}, u32[]{:S(2)}, u32[]{:S(2)}) collective-permute-start(bf16[1,256,512]{1,2,0:T(8,128)(2,1)S(1)} %get-tuple-element.152), channel_id=1, source_target_pairs={{16,0},{20,4},{24,8},{28,12},{17,1},{21,5},{25,9},{29,13},{18,2},{... | collective-permute-start | bytes 786440 | tf_op jit(solution)/shard_map/ppermute | solution.py:292
  177.5 36.4 %collective-permute-start.6 = (bf16[1,256,512]{1,2,0:T(8,128)(2,1)S(1)}, bf16[1,256,512]{1,2,0:T(8,128)(2,1)S(1)}, u32[]{:S(2)}, u32[]{:S(2)}) collective-permute-start(bf16[1,256,512]{1,2,0:T(8,128)(2,1)S(1)} %get-tuple-element.153), channel_id=1, source_target_pairs={{12,0},{16,4},{20,8},{24,12},{28,16},{13,1},{17,5},{21,9},{25,13},... | collective-permute-start | bytes 786440 | tf_op jit(solution)/shard_map/ppermute | solution.py:292
  178.8 35.1 %collective-permute-start.5 = (bf16[1,256,512]{1,2,0:T(8,128)(2,1)S(1)}, bf16[1,256,512]{1,2,0:T(8,128)(2,1)S(1)}, u32[]{:S(2)}, u32[]{:S(2)}) collective-permute-start(bf16[1,256,512]{1,2,0:T(8,128)(2,1)S(1)} %get-tuple-element.154), channel_id=1, source_target_pairs={{8,0},{12,4},{16,8},{20,12},{24,16},{28,20},{9,1},{13,5},{17,9},{2... | collective-permute-start | bytes 786440 | tf_op jit(solution)/shard_map/ppermute | solution.py:292
  214.0 1.6 copy-start.5
  216.6 69.6 %copy-start.6 = (bf16[1,256,2048]{2,1,0:T(8,128)(2,1)S(1)}, bf16[1,256,2048]{2,1,0:T(8,128)(2,1)}, u32[]{:S(2)}) copy-start(bf16[1,256,2048]{2,1,0:T(8,128)(2,1)} %param.11) | copy-start | bytes 3145732
  (1 other events, 0.8 us)

commit v2 on v1

--- a/solution.py
+++ b/solution.py
@@ -111,13 +111,15 @@
         functools.partial(gather_kernel, count),
         out_shape=shapes,
         in_specs=[pl.BlockSpec(memory_space=pl.ANY)] * 3,
-        out_specs=[pl.BlockSpec(memory_space=pl.ANY)] * 3,
+        out_specs=[pl.BlockSpec(memory_space=pltpu.VMEM)] * 3,
         scratch_shapes=[
             pltpu.SemaphoreType.DMA((3,)),
             pltpu.SemaphoreType.DMA((slots,)),
             pltpu.SemaphoreType.DMA((slots,)),
         ],
-        compiler_params=pltpu.CompilerParams(collective_id=0, has_side_effects=True),
+        compiler_params=pltpu.CompilerParams(
+            collective_id=0, has_side_effects=True, vmem_limit_bytes=40 * 1024 * 1024
+        ),
         name="gather_weights",
     )(w_q, w_kv, w_out)
 
@@ -298,77 +300,112 @@
     return (values * inv_rms, inv_rms)
 
 
-def head_block(items, allowed):
-    quer3, keys2, vals2, grad3 = items
+def attend_kernel(preds, q_ref, g_ref, *refs):
+    count = preds + 1
+    keys, values, refs = (refs[:count], refs[count : 2 * count], refs[2 * count :])
+    attended_ref, dq_ref, dkv_refs, refs = (refs[0], refs[1], refs[2 : 2 + count], refs[2 + count :])
+    bias, work, dk_acc, dv_acc = refs
+    shard = q_ref.shape[0]
+    group = pl.program_id(0)
+    heads = q_ref.shape[1] // HEAD_SIZE
     scale = 1.0 / math.sqrt(HEAD_SIZE)
-    scores = jnp.einsum("imd,jd->mij", quer3, keys2, preferred_element_type=jnp.float32) * scale
-    scores = jnp.where(allowed[None], scores, -jnp.inf)
-    top = jnp.max(scores, axis=-1, keepdims=True)
-    expo = jnp.exp(scores - top)
-    probs = expo / jnp.sum(expo, axis=-1, keepdims=True)
-    probs_low = probs.astype(jnp.bfloat16)
-    attended = jnp.einsum("mij,jd->imd", probs_low, vals2, preferred_element_type=jnp.float32)
-    grad_probs = jnp.einsum("imd,jd->mij", grad3, vals2, preferred_element_type=jnp.float32)
-    delta = jnp.einsum("imd,imd->mi", grad3.astype(jnp.float32), attended)
-    grad_scores = (probs * (grad_probs - delta[..., None]) * scale).astype(jnp.bfloat16)
-    grad_query = jnp.einsum("mij,jd->imd", grad_scores, keys2, preferred_element_type=jnp.float32)
-    key_gradient = jnp.einsum("mij,imd->jd", grad_scores, quer3, preferred_element_type=jnp.float32)
-    value_gradient = jnp.einsum("mij,imd->jd", probs_low, grad3, preferred_element_type=jnp.float32)
-    return (
-        attended.astype(jnp.bfloat16),
-        grad_query.astype(jnp.bfloat16),
-        key_gradient.astype(jnp.bfloat16),
-        value_gradient.astype(jnp.bfloat16),
-    )
-
-
-def window_block(query_rows, key_value_pairs, output_gradient, base):
-    window_extent = key_value_pairs.shape[0]
-    element_count = query_rows.shape[0]
-    query_group = QUERY_HEADS // KEY_VALUE_HEADS
-    query_pos = base + jnp.arange(element_count, dtype=jnp.int32)
-    key_pos = base - WINDOW_TOKENS + jnp.arange(window_extent, dtype=jnp.int32)
-    offset = query_pos[:, None] - key_pos[None, :]
-    allowed = (offset >= 0) & (offset < WINDOW_TOKENS) & (key_pos[None, :] >= 0)
-    query_grouped = query_rows.reshape(
-        element_count, KEY_VALUE_HEADS, query_group, HEAD_SIZE
-    ).transpose(1, 0, 2, 3)
-    gradient_grouped = output_gradient.reshape(
-        element_count, KEY_VALUE_HEADS, query_group, HEAD_SIZE
-    ).transpose(1, 0, 2, 3)
-    key_tensor = (
-        key_value_pairs[:, : KEY_VALUE_HEADS * HEAD_SIZE]
-        .reshape(window_extent, KEY_VALUE_HEADS, HEAD_SIZE)
-        .transpose(1, 0, 2)
-    )
-    value_tensor = (
-        key_value_pairs[:, KEY_VALUE_HEADS * HEAD_SIZE :]
-        .reshape(window_extent, KEY_VALUE_HEADS, HEAD_SIZE)
-        .transpose(1, 0, 2)
-    )
-
-    def per_head(items):
-        return head_block(items, allowed)
-
-    attended, grad_query, key_gradient, value_gradient = lax.map(
-        per_head, (query_grouped, key_tensor, value_tensor, gradient_grouped)
-    )
-    attended = attended.transpose(1, 0, 2, 3).reshape(element_count, QUERY_HEADS * HEAD_SIZE)
-    grad_query = grad_query.transpose(1, 0, 2, 3).reshape(element_count, QUERY_HEADS * HEAD_SIZE)
-    key_gradient = key_gradient.transpose(1, 0, 2).reshape(
-        window_extent, KEY_VALUE_HEADS * HEAD_SIZE
-    )
-    value_gradient = value_gradient.transpose(1, 0, 2).reshape(
-        window_extent, KEY_VALUE_HEADS * HEAD_SIZE
-    )
-    value_partial_sum = jnp.concatenate([key_gradient, value_gradient], 1)
-    return (attended, grad_query, value_partial_sum)
+    contract_last = (((1,), (1,)), ((), ()))
+    contract_mid = (((1,), (0,)), ((), ()))
+
+    def dot(a, b, dims):
+        return lax.dot_general(a, b, dims, preferred_element_type=jnp.float32)
+
+    @pl.when(group == 0)
+    def _():
+        base = lax.axis_index("ctx") * shard
+        key_at = lax.broadcasted_iota(jnp.int32, (shard, shard), 0)
+        query_at = lax.broadcasted_iota(jnp.int32, (shard, shard), 1)
+        for block in range(count):
+            key_pos = key_at + (block - preds) * shard
+            offset = query_at - key_pos
+            allowed = (offset >= 0) & (offset < WINDOW_TOKENS) & (key_pos + base >= 0)
+            bias[block] = jnp.where(allowed, 0.0, -jnp.inf)
+
+    keys_t = [k[...].T for k in keys]
+    values_t = [v[...].T for v in values]
+    for head in range(heads):
+        columns = slice(head * HEAD_SIZE, (head + 1) * HEAD_SIZE)
+        q = q_ref[:, columns]
+        g = g_ref[:, columns]
+        slot = head % 2
+        top = None
+        for block in range(count):
+            scores = dot(keys[block][...], q, contract_last) * (scale * math.log2(math.e))
+            scores = scores + bias[block]
+            work[slot, block] = scores
+            peak = jnp.max(scores, axis=0, keepdims=True)
+            top = peak if top is None else jnp.maximum(top, peak)
+        total = 0.0
+        for block in range(count):
+            expo = jnp.exp2(work[slot, block] - top)
+            work[slot, block] = expo
+            total = total + jnp.sum(expo, axis=0, keepdims=True)
+        inverse = 1.0 / total
+        attended_t = 0.0
+        for block in range(count):
+            probs = work[slot, block] * inverse
+            work[slot, block] = probs
+            probs_low = probs.astype(jnp.bfloat16)
+            attended_t = attended_t + dot(values_t[block], probs_low, contract_mid)
+            dv = dot(probs_low, g, contract_mid)
+            dv_acc[block] = dv if head == 0 else dv_acc[block] + dv
+        delta = jnp.sum(g.astype(jnp.float32).T * attended_t, axis=0, keepdims=True)
+        attended_ref[:, columns] = attended_t.T.astype(jnp.bfloat16)
+        dq_t = 0.0
+        for block in range(count):
+            grad_probs = dot(values[block][...], g, contract_last)
+            grad_scores = work[slot, block] * (grad_probs - delta) * scale
+            grad_scores = grad_scores.astype(jnp.bfloat16)
+            dq_t = dq_t + dot(keys_t[block], grad_scores, contract_mid)
+            dk = dot(grad_scores, q, contract_mid)
+            dk_acc[block] = dk if head == 0 else dk_acc[block] + dk
+        dq_ref[:, columns] = dq_t.T.astype(jnp.bfloat16)
+    for block in range(count):
+        at = pl.multiple_of(group * HEAD_SIZE, HEAD_SIZE)
+        dkv_refs[block][:, pl.ds(at, HEAD_SIZE)] = dk_acc[block].astype(jnp.bfloat16)
+        at = pl.multiple_of((KEY_VALUE_HEADS + group) * HEAD_SIZE, HEAD_SIZE)
+        dkv_refs[block][:, pl.ds(at, HEAD_SIZE)] = dv_acc[block].astype(jnp.bfloat16)
+
+
+def attend(query_rows, grad_rows, blocks):
+    shard, width = query_rows.shape
+    count = len(blocks)
+    group_width = width // KEY_VALUE_HEADS
+    query_spec = pl.BlockSpec((shard, group_width), lambda i: (0, i))
+    key_spec = pl.BlockSpec((shard, HEAD_SIZE), lambda i: (0, i))
+    value_spec = pl.BlockSpec((shard, HEAD_SIZE), lambda i: (0, KEY_VALUE_HEADS + i))
+    pair_spec = pl.BlockSpec((shard, blocks[0].shape[1]), lambda i: (0, 0))
+    wide = jax.ShapeDtypeStruct((shard, width), jnp.bfloat16)
+    pair = jax.ShapeDtypeStruct(blocks[0].shape, jnp.bfloat16)
+    flops = 10 * shard * shard * count * width
+    return pl.pallas_call(
+        functools.partial(attend_kernel, count - 1),
+        grid=(KEY_VALUE_HEADS,),
+        out_shape=[wide, wide] + [pair] * count,
+        in_specs=[query_spec] * 2 + [key_spec] * count + [value_spec] * count,
+        out_specs=[query_spec] * 2 + [pair_spec] * count,
+        scratch_shapes=[
+            pltpu.VMEM((count, shard, shard), jnp.float32),
+            pltpu.VMEM((2, count, shard, shard), jnp.float32),
+            pltpu.VMEM((count, shard, HEAD_SIZE), jnp.float32),
+            pltpu.VMEM((count, shard, HEAD_SIZE), jnp.float32),
+        ],
+        compiler_params=pltpu.CompilerParams(vmem_limit_bytes=40 * 1024 * 1024),
+        cost_estimate=pl.CostEstimate(
+            flops=flops, bytes_accessed=4 * 1024 * 1024, transcendentals=shard * shard * count * 8
+        ),
+        name="attend",
+    )(query_rows, grad_rows, *blocks, *blocks)
 
 
 def shards(x_cur, x_next, cot_cur, cot_next, w_q, w_kv, w_out):
     full_q, full_kv, full_out = gather_weights(w_q, w_kv, w_out)
     seq_count, shard, width = x_cur.shape
-    base = lax.axis_index("ctx") * shard
     preds = WINDOW_TOKENS // shard
     normed, inv_rms = normalize(x_cur)
     hidden = normed.astype(jnp.bfloat16)
@@ -384,21 +421,14 @@
     earlier = []
     for hop in range(1, preds + 1):
         earlier.append(from_behind(key_value_pairs, "ctx", hop))
-    window_keys = jnp.concatenate(earlier[::-1] + [key_value_pairs], axis=1)
-
-    def per_sequence(items):
-        q_rows, kv_rows, g_rows = items
-        return window_block(q_rows, kv_rows, g_rows, base)
-
-    attended, grad_query, value_partial_sum = lax.map(
-        per_sequence, (query_rows, window_keys, grad_attn)
-    )
-    owned = value_partial_sum[:, WINDOW_TOKENS:].astype(jnp.float32)
+    results = []
+    for seq in range(seq_count):
+        window = [block[seq] for block in earlier[::-1]] + [key_value_pairs[seq]]
+        results.append(attend(query_rows[seq], grad_attn[seq], window))
+    attended, grad_query, *pieces = (jnp.stack(parts) for parts in zip(*results))
+    owned = pieces[preds].astype(jnp.float32)
     for hop in range(1, preds + 1):
-        piece = value_partial_sum[
-            :, WINDOW_TOKENS - hop * shard : WINDOW_TOKENS - (hop - 1) * shard
-        ]
-        owned = owned + from_behind(piece, "ctx", -hop).astype(jnp.float32)
+        owned = owned + from_behind(pieces[preds - hop], "ctx", -hop).astype(jnp.float32)
     grad_kv = owned.astype(jnp.bfloat16)
     layer_out = jnp.einsum("sic,dc->sid", attended, full_out, preferred_element_type=jnp.float32)
     x_prev = (x_next.astype(jnp.float32) - 2.0 * layer_out).astype(jnp.bfloat16)

time: 290 us -> 208 us (0.72)
  the two profiles are of different devices: /device:TPU:0 before, /device:TPU:8 now
where the time goes in v2:
time: 208 us
  Pallas kernels  129 us (62%)
  waiting for transfers between devices  41.3 us (20%)
  starting transfers between devices  17.7 us (9%)
  matrix products  11.3 us (5%)
  local copies, waits for them, and re-layouts  4.35 us (2%)
  other arithmetic  3.41 us (2%)
    pallas_call x1, Pallas kernels, reduce_terms(): pl.pallas_call(functools.partial(reduce_kernel, ctx_count, fsdp_count, pa...  73.5 us
    ppermute x8, waiting for transfers between devices, from_behind(): lax.ppermute(value, axis, [(source, source + steps) for source in range(l...  41.3 us
    pallas_call x1, Pallas kernels, gather_weights(): pl.pallas_call(functools.partial(gather_kernel, count), out_shape=shapes,...  40 us
    ppermute x8, starting transfers between devices, from_behind(): lax.ppermute(value, axis, [(source, source + steps) for source in range(l...  17.7 us
    pallas_call x1, Pallas kernels, attend(): pl.pallas_call(functools.partial(attend_kernel, count - 1), grid=(KEY_VAL...  15.4 us
    unnamed x15, local copies, waits for them, and re-layouts  4.35 us
  transfers between devices with their start and end apart: 8, of which 4 were waited for; matrix products, arithmetic and copies ran while one was open for 4% of the time, Pallas kernels for 0%

profile of v2, /device:TPU:8, one launch (start us, length us, event | category | flops | bytes accessed | tf_op | source)
XLA Modules:
  0.0 207.7 jit_solution(2077509786940803546)
XLA Ops:
  0.6 0.0 copy-start
  0.7 1.7 fusion.13
  2.3 1.2 copy-done.1
  3.6 1.2 copy-done.2
  4.8 1.0 copy-done.3
  5.8 40.0 %gather_weights.1 = (bf16[2048,1024]{1,0:T(8,128)(2,1)S(1)}, bf16[2048,512]{1,0:T(8,128)(2,1)S(1)}, bf16[2048,1024]{1,0:T(8,128)(2,1)S(1)}) custom-call(bf16[512,1024]{1,0:T(8,128)(2,1)S(1)} %copy-done.1, bf16[512,512]{1,0:T(8,128)(2,1)S(1)} %copy-done.3, bf16[512,1024]{1,0:T(8,128)(2,1)S(1)} %copy-done.2), custom_call_target="tpu_custom_call" | custom-call | tf_op jit(solution)/shard_map/gather_weights/pallas_call | solution.py:110
  45.8 0.7 convolution_convert_fusion.3.refs_4_.refs_9_
  46.6 2.6 %collective-permute-start.3 = (bf16[1,256,512]{2,1,0:T(8,128)(2,1)S(1)}, bf16[1,256,512]{2,1,0:T(8,128)(2,1)S(1)}, u32[]{:S(2)}, u32[]{:S(2)}) collective-permute-start(bf16[1,256,512]{2,1,0:T(8,128)(2,1)S(1)} %bitcast.51), channel_id=1, source_target_pairs={{0,4},{4,8},{8,12},{12,16},{16,20},{20,24},{24,28},{1,5},{5,9},{9,... | collective-permute-start | bytes 786440 | tf_op jit(solution)/shard_map/ppermute | solution.py:294
  49.1 3.5 %collective-permute-start.2 = (bf16[1,256,512]{2,1,0:T(8,128)(2,1)S(1)}, bf16[1,256,512]{2,1,0:T(8,128)(2,1)S(1)}, u32[]{:S(2)}, u32[]{:S(2)}) collective-permute-start(bf16[1,256,512]{2,1,0:T(8,128)(2,1)S(1)} %bitcast.52), channel_id=1, source_target_pairs={{0,8},{4,12},{8,16},{12,20},{16,24},{20,28},{1,9},{5,13},{9,17},{1... | collective-permute-start | bytes 786440 | tf_op jit(solution)/shard_map/ppermute | solution.py:294
  52.6 3.7 %collective-permute-start.1 = (bf16[1,256,512]{2,1,0:T(8,128)(2,1)S(1)}, bf16[1,256,512]{2,1,0:T(8,128)(2,1)S(1)}, u32[]{:S(2)}, u32[]{:S(2)}) collective-permute-start(bf16[1,256,512]{2,1,0:T(8,128)(2,1)S(1)} %bitcast.53), channel_id=1, source_target_pairs={{0,12},{4,16},{8,20},{12,24},{16,28},{1,13},{5,17},{9,21},{13,25},... | collective-permute-start | bytes 786440 | tf_op jit(solution)/shard_map/ppermute | solution.py:294
  56.4 1.3 collective-permute-start
  57.7 1.3 convolution_convert_fusion.2.q_ref
  59.0 1.2 fusion.15.g_ref
  60.3 10.2 %collective-permute-done.1 = bf16[1,256,512]{2,1,0:T(8,128)(2,1)S(1)} collective-permute-done((bf16[1,256,512]{2,1,0:T(8,128)(2,1)S(1)}, bf16[1,256,512]{2,1,0:T(8,128)(2,1)S(1)}, u32[]{:S(2)}, u32[]{:S(2)}) %collective-permute-start.1) | collective-permute-done | bytes 262176 | tf_op jit(solution)/shard_map/ppermute | solution.py:294
  70.5 4.8 %collective-permute-done = bf16[1,256,512]{2,1,0:T(8,128)(2,1)S(1)} collective-permute-done((bf16[1,256,512]{2,1,0:T(8,128)(2,1)S(1)}, bf16[1,256,512]{2,1,0:T(8,128)(2,1)S(1)}, u32[]{:S(2)}, u32[]{:S(2)}) %collective-permute-start) | collective-permute-done | bytes 262176 | tf_op jit(solution)/shard_map/ppermute | solution.py:294
  75.3 15.4 %attend.1 = (bf16[256,1024]{1,0:T(8,128)(2,1)S(1)}, bf16[256,1024]{1,0:T(8,128)(2,1)S(1)}, bf16[256,512]{1,0:T(8,128)(2,1)S(1)}, bf16[256,512]{1,0:T(8,128)(2,1)...) custom-call(bf16[256,1024]{1,0:T(8,128)(2,1)S(1)} %convolution_convert_fusion.2.q_ref, ...), custom_call_target="tpu_custom_call" | custom-call | flops 3355443200 | bytes 4194304 | tf_op jit(solution)/shard_map/attend/pallas_call | solution.py:386
  90.7 1.9 collective-permute-start.4
  92.6 1.9 collective-permute-start.5
  94.6 1.3 collective-permute-start.6
  95.9 1.5 collective-permute-start.7
  97.4 1.4 convolution_convert_fusion.refs_0_
  98.8 2.3 %fusion.7 = bf16[1,256,2048]{2,1,0:T(8,128)(2,1)} fusion(bf16[256,1024]{1,0:T(8,128)(2,1)S(1)} %get-tuple-element.16, bf16[2048,1024]{1,0:T(8,128)(2,1)S(1)} %get-tuple-element.14, bf16[1,256,2048]{2,1,0:T(8,128)(2,1)S(1)} %copy-done.6), kind=kOutput, calls=%fused_computation.14 | convolution fusion | flops 1075838976 | bytes 6815744 | tf_op jit(solution)/shard_map/sic,dc->sid/dot_general | solution.py:433
  101.0 1.3 fusion.refs_2_
  102.3 6.8 %collective-permute-done.4 = bf16[1,256,512]{2,1,0:T(8,128)(2,1)S(1)} collective-permute-done((bf16[1,256,512]{2,1,0:T(8,128)(2,1)S(1)}, bf16[1,256,512]{2,1,0:T(8,128)(2,1)S(1)}, u32[]{:S(2)}, u32[]{:S(2)}) %collective-permute-start.4) | collective-permute-done | bytes 262176 | tf_op jit(solution)/shard_map/ppermute | solution.py:294
  109.1 19.4 %collective-permute-done.5 = bf16[1,256,512]{2,1,0:T(8,128)(2,1)S(1)} collective-permute-done((bf16[1,256,512]{2,1,0:T(8,128)(2,1)S(1)}, bf16[1,256,512]{2,1,0:T(8,128)(2,1)S(1)}, u32[]{:S(2)}, u32[]{:S(2)}) %collective-permute-start.5) | collective-permute-done | bytes 262176 | tf_op jit(solution)/shard_map/ppermute | solution.py:294
  128.5 0.2 fusion.23
  128.7 0.7 fusion.28
  129.5 0.8 convolution_convert_fusion.1.refs_1_
  130.3 1.5 fusion.8
  131.8 73.5 %reduce_terms.1 = f32[64,2560]{1,0:T(8,128)S(1)} custom-call(bf16[2048,1024]{1,0:T(8,128)(2,1)S(1)} %convolution_convert_fusion.refs_0_, bf16[2048,512]{1,0:T(8,128)(2,1)S(1)} %convolution_convert_fusion.1.refs_1_, bf16[2048,1024]{1,0:T(8,128)(2,1)S(1)} %fusion.refs_2_), custom_call_target="tpu_custom_call" | custom-call | tf_op jit(solution)/shard_map/reduce_terms/pallas_call | solution.py:278
  205.3 1.6 fusion.12
  206.9 0.8 copy.15
  (16 shorter events, 0.1 us)
Async XLA Ops:
  0.6 58.4 %copy-start = (bf16[1,256,2048]{2,1,0:T(8,128)(2,1)S(1)}, bf16[1,256,2048]{2,1,0:T(8,128)(2,1)}, u32[]{:S(2)}) copy-start(bf16[1,256,2048]{2,1,0:T(8,128)(2,1)} %param.10) | copy-start | bytes 3145732
  0.6 45.2 %copy-start.4 = (bf16[1,256,2048]{2,1,0:T(8,128)(2,1)S(1)}, bf16[1,256,2048]{2,1,0:T(8,128)(2,1)}, u32[]{:S(2)}) copy-start(bf16[1,256,2048]{2,1,0:T(8,128)(2,1)} %param.7) | copy-start | bytes 3145732
  2.3 1.2 copy-start.1
  3.6 1.2 copy-start.2
  4.8 1.0 copy-start.3
  46.6 13.7 %collective-permute-start.3 = (bf16[1,256,512]{2,1,0:T(8,128)(2,1)S(1)}, bf16[1,256,512]{2,1,0:T(8,128)(2,1)S(1)}, u32[]{:S(2)}, u32[]{:S(2)}) collective-permute-start(bf16[1,256,512]{2,1,0:T(8,128)(2,1)S(1)} %bitcast.51), channel_id=1, source_target_pairs={{0,4},{4,8},{8,12},{12,16},{16,20},{20,24},{24,28},{1,5},{5,9},{9,... | collective-permute-start | bytes 786440 | tf_op jit(solution)/shard_map/ppermute | solution.py:294
  49.1 11.1 %collective-permute-start.2 = (bf16[1,256,512]{2,1,0:T(8,128)(2,1)S(1)}, bf16[1,256,512]{2,1,0:T(8,128)(2,1)S(1)}, u32[]{:S(2)}, u32[]{:S(2)}) collective-permute-start(bf16[1,256,512]{2,1,0:T(8,128)(2,1)S(1)} %bitcast.52), channel_id=1, source_target_pairs={{0,8},{4,12},{8,16},{12,20},{16,24},{20,28},{1,9},{5,13},{9,17},{1... | collective-permute-start | bytes 786440 | tf_op jit(solution)/shard_map/ppermute | solution.py:294
  52.6 17.9 %collective-permute-start.1 = (bf16[1,256,512]{2,1,0:T(8,128)(2,1)S(1)}, bf16[1,256,512]{2,1,0:T(8,128)(2,1)S(1)}, u32[]{:S(2)}, u32[]{:S(2)}) collective-permute-start(bf16[1,256,512]{2,1,0:T(8,128)(2,1)S(1)} %bitcast.53), channel_id=1, source_target_pairs={{0,12},{4,16},{8,20},{12,24},{16,28},{1,13},{5,17},{9,21},{13,25},... | collective-permute-start | bytes 786440 | tf_op jit(solution)/shard_map/ppermute | solution.py:294
  56.4 19.0 %collective-permute-start = (bf16[1,256,512]{2,1,0:T(8,128)(2,1)S(1)}, bf16[1,256,512]{2,1,0:T(8,128)(2,1)S(1)}, u32[]{:S(2)}, u32[]{:S(2)}) collective-permute-start(bf16[1,256,512]{2,1,0:T(8,128)(2,1)S(1)} %bitcast.54), channel_id=1, source_target_pairs={{0,16},{4,20},{8,24},{12,28},{1,17},{5,21},{9,25},{13,29},{2,18},{... | collective-permute-start | bytes 786440 | tf_op jit(solution)/shard_map/ppermute | solution.py:294
  90.7 18.4 %collective-permute-start.4 = (bf16[1,256,512]{2,1,0:T(8,128)(2,1)S(1)}, bf16[1,256,512]{2,1,0:T(8,128)(2,1)S(1)}, u32[]{:S(2)}, u32[]{:S(2)}) collective-permute-start(bf16[1,256,512]{2,1,0:T(8,128)(2,1)S(1)} %bitcast.58), channel_id=1, source_target_pairs={{4,0},{8,4},{12,8},{16,12},{20,16},{24,20},{28,24},{5,1},{9,5},{13... | collective-permute-start | bytes 786440 | tf_op jit(solution)/shard_map/ppermute | solution.py:294
  92.6 35.9 %collective-permute-start.5 = (bf16[1,256,512]{2,1,0:T(8,128)(2,1)S(1)}, bf16[1,256,512]{2,1,0:T(8,128)(2,1)S(1)}, u32[]{:S(2)}, u32[]{:S(2)}) collective-permute-start(bf16[1,256,512]{2,1,0:T(8,128)(2,1)S(1)} %bitcast.55), channel_id=1, source_target_pairs={{8,0},{12,4},{16,8},{20,12},{24,16},{28,20},{9,1},{13,5},{17,9},{2... | collective-permute-start | bytes 786440 | tf_op jit(solution)/shard_map/ppermute | solution.py:294
  94.6 34.0 %collective-permute-start.6 = (bf16[1,256,512]{2,1,0:T(8,128)(2,1)S(1)}, bf16[1,256,512]{2,1,0:T(8,128)(2,1)S(1)}, u32[]{:S(2)}, u32[]{:S(2)}) collective-permute-start(bf16[1,256,512]{2,1,0:T(8,128)(2,1)S(1)} %bitcast.50), channel_id=1, source_target_pairs={{12,0},{16,4},{20,8},{24,12},{28,16},{13,1},{17,5},{21,9},{25,13},... | collective-permute-start | bytes 786440 | tf_op jit(solution)/shard_map/ppermute | solution.py:294
  95.9 32.7 %collective-permute-start.7 = (bf16[1,256,512]{2,1,0:T(8,128)(2,1)S(1)}, bf16[1,256,512]{2,1,0:T(8,128)(2,1)S(1)}, u32[]{:S(2)}, u32[]{:S(2)}) collective-permute-start(bf16[1,256,512]{2,1,0:T(8,128)(2,1)S(1)} %bitcast.49), channel_id=1, source_target_pairs={{16,0},{20,4},{24,8},{28,12},{17,1},{21,5},{25,9},{29,13},{18,2},{... | collective-permute-start | bytes 786440 | tf_op jit(solution)/shard_map/ppermute | solution.py:294
  97.4 1.4 copy-start.6
  131.8 73.5 %copy-start.5 = (bf16[1,256,2048]{2,1,0:T(8,128)(2,1)S(1)}, bf16[1,256,2048]{2,1,0:T(8,128)(2,1)}, u32[]{:S(2)}) copy-start(bf16[1,256,2048]{2,1,0:T(8,128)(2,1)} %param.9) | copy-start | bytes 3145732

commit v3 on v2

--- a/solution.py
+++ b/solution.py
@@ -136,18 +136,24 @@
 
 def reduce_parts(widths):
     q_width, kv_width, o_width = widths
-    tail = 128
+    tail = 256
+    half = kv_width // 2
     return (
         (0, 0, q_width - tail, 0),
         (2, 0, o_width - tail, 1),
-        (1, 0, kv_width, 2),
         (0, q_width - tail, tail, 2),
         (2, o_width - tail, tail, 2),
-    )
-
-
-def reduce_kernel(ctx_count, fsdp_count, parts, scale, *refs):
-    terms, out_ref, refs = (refs[:3], refs[3], refs[4:])
+        (1, 0, half, 0),
+        (1, half, half, 1),
+    )
+
+
+def reduce_kernel(ctx_count, fsdp_count, preds, parts, scale, *refs):
+    term_q, term_o, hidden_ref, refs = (refs[0], refs[1], refs[2], refs[3:])
+    pieces, out_ref, grad_kv_ref, refs = (refs[: preds + 1], refs[preds + 1], refs[preds + 2], refs[preds + 3 :])
+    arrived, kv_sum, term_kv, kv_send, kv_recv = refs[:5]
+    refs = refs[5:]
+    terms = (term_q, term_kv, term_o)
     core, *orders = reduce_plan(ctx_count, fsdp_count)
     stages = len(orders[0])
     accs, recvs = ([], [])
@@ -171,10 +177,34 @@
     barrier = pltpu.get_barrier_semaphore()
     for bit in [core] + orders[0]:
         pl.semaphore_signal(barrier, inc=1, device_id=partner(bit), device_id_type=MESH)
-    pl.semaphore_wait(barrier, stages + 1)
+    ctx_at = place["ctx"]
+    for hop in range(1, preds + 1):
+
+        @pl.when(ctx_at + hop < ctx_count)
+        def _():
+            pl.semaphore_signal(
+                barrier, inc=1, device_id=(ctx_at + hop, place["fsdp"]), device_id_type=MESH
+            )
+
+    pl.semaphore_wait(barrier, stages + 1 + jnp.minimum(ctx_at, preds))
+
+    def piece_copy(hop, target):
+        return pltpu.make_async_remote_copy(
+            src_ref=pieces[preds - hop], dst_ref=arrived.at[hop - 1],
+            send_sem=kv_send.at[hop - 1], recv_sem=kv_recv.at[hop - 1],
+            device_id=(target, place["fsdp"]), device_id_type=MESH,
+        )
+
+    for hop in range(1, preds + 1):
+
+        @pl.when(ctx_at >= hop)
+        def _():
+            piece_copy(hop, ctx_at - hop).start()
 
     half_blocks = count // 2
-    for p, (index, start, width, order) in enumerate(parts):
+
+    def launch(p):
+        index, start, width, order = parts[p]
         columns = pl.ds(start, width)
 
         def one(j, carry):
@@ -216,10 +246,45 @@
         lax.fori_loop(0, size // step, body, 0)
 
     half_rows = half_blocks * block
+    early = [p for p, part in enumerate(parts) if part[0] != 1]
+    late = [p for p, part in enumerate(parts) if part[0] == 1]
+    for p in early:
+        launch(p)
+
+    def own_keys():
+        kv_sum[...] = pieces[preds][...].astype(jnp.float32)
+        for hop in range(1, preds + 1):
+
+            @pl.when(ctx_at + hop < ctx_count)
+            def _():
+                piece_copy(hop, ctx_at + hop).wait_recv()
+                kv_sum[...] += arrived[hop - 1].astype(jnp.float32)
+
+        grad_kv_ref[...] = kv_sum[...].astype(jnp.bfloat16)
+        step = 256
+
+        def body(i, carry):
+            at = pl.ds(pl.multiple_of(i * step, step), step)
+            term_kv[at] = lax.dot_general(
+                hidden_ref[:, at], grad_kv_ref[...], (((0,), (0,)), ((), ())),
+                preferred_element_type=jnp.float32,
+            ).astype(jnp.bfloat16)
+            return carry
+
+        lax.fori_loop(0, term_kv.shape[0] // step, body, 0)
+        for p in late:
+            launch(p)
+
+    lag = 2
     sends, latest = ([], {})
-    for stage in range(stages + 1):
-        size = half_rows >> stage
+    for turn in range(stages + 1 + lag):
+        if turn == lag:
+            own_keys()
         for p, (index, start, width, order) in enumerate(parts):
+            stage = turn - lag if p in late else turn
+            if stage < 0 or stage > stages:
+                continue
+            size = half_rows >> stage
             if stage == 0:
                 whole = terms[index].at[pl.ds(0, half_rows), pl.ds(start, width)]
                 pltpu.make_async_copy(whole, accs[p][0], own_sem.at[p]).wait()
@@ -253,17 +318,28 @@
                 sends.append(copy)
     for copy in sends:
         copy.wait_send()
-
-
-def reduce_terms(term_q, term_kv, term_o, scale):
+    for hop in range(1, preds + 1):
+
+        @pl.when(ctx_at >= hop)
+        def _():
+            piece_copy(hop, ctx_at - hop).wait_send()
+
+
+def reduce_terms(term_q, term_o, hidden, pieces, scale):
     ctx_count, fsdp_count = (lax.axis_size("ctx"), lax.axis_size("fsdp"))
-    terms = (term_q, term_kv, term_o)
-    widths = [t.shape[1] for t in terms]
+    preds = len(pieces) - 1
+    widths = [term_q.shape[1], pieces[0].shape[1], term_o.shape[1]]
     parts = reduce_parts(widths)
     count = ctx_count * fsdp_count
     block = term_q.shape[0] // count
     stages = count.bit_length() - 2
-    scratch = []
+    scratch = [
+        pltpu.VMEM((preds,) + pieces[0].shape, jnp.bfloat16),
+        pltpu.VMEM(pieces[0].shape, jnp.float32),
+        pltpu.VMEM((term_q.shape[0], widths[1]), jnp.bfloat16),
+        pltpu.SemaphoreType.DMA((preds,)),
+        pltpu.SemaphoreType.DMA((preds,)),
+    ]
     for _, _, width, _ in parts:
         half_rows = count // 2 * block
         for stage in range(stages):
@@ -276,16 +352,20 @@
         pltpu.SemaphoreType.DMA((len(parts), stages + 1)),
     ]
     return pl.pallas_call(
-        functools.partial(reduce_kernel, ctx_count, fsdp_count, parts, scale),
-        out_shape=jax.ShapeDtypeStruct((block, sum(widths)), jnp.float32),
-        in_specs=[pl.BlockSpec(memory_space=pl.ANY)] * 3,
-        out_specs=pl.BlockSpec(memory_space=pltpu.VMEM),
+        functools.partial(reduce_kernel, ctx_count, fsdp_count, preds, parts, scale),
+        out_shape=[
+            jax.ShapeDtypeStruct((block, sum(widths)), jnp.float32),
+            jax.ShapeDtypeStruct(pieces[0].shape, jnp.bfloat16),
+        ],
+        in_specs=[pl.BlockSpec(memory_space=pl.ANY)] * 2
+        + [pl.BlockSpec(memory_space=pltpu.VMEM)] * (preds + 2),
+        out_specs=[pl.BlockSpec(memory_space=pltpu.VMEM)] * 2,
         scratch_shapes=scratch,
         compiler_params=pltpu.CompilerParams(
             collective_id=1, has_side_effects=True, vmem_limit_bytes=40 * 1024 * 1024
         ),
         name="reduce_terms",
-    )(*terms)
+    )(term_q, term_o, hidden, *pieces)
 
 
 def from_behind(value, axis, steps):
@@ -426,42 +506,38 @@
         window = [block[seq] for block in earlier[::-1]] + [key_value_pairs[seq]]
         results.append(attend(query_rows[seq], grad_attn[seq], window))
     attended, grad_query, *pieces = (jnp.stack(parts) for parts in zip(*results))
-    owned = pieces[preds].astype(jnp.float32)
-    for hop in range(1, preds + 1):
-        owned = owned + from_behind(pieces[preds - hop], "ctx", -hop).astype(jnp.float32)
-    grad_kv = owned.astype(jnp.bfloat16)
     layer_out = jnp.einsum("sic,dc->sid", attended, full_out, preferred_element_type=jnp.float32)
     x_prev = (x_next.astype(jnp.float32) - 2.0 * layer_out).astype(jnp.bfloat16)
-    grad_hidden = jnp.einsum("sic,dc->sid", grad_query, full_q, preferred_element_type=jnp.float32)
-    grad_hidden = grad_hidden + jnp.einsum(
-        "sic,dc->sid", grad_kv, full_kv, preferred_element_type=jnp.float32
-    )
-    grad_x = inv_rms * (
-        grad_hidden - normed * jnp.mean(grad_hidden * normed, axis=-1, keepdims=True)
-    )
-    grad_cur = (cot_cur.astype(jnp.float32) + grad_x).astype(jnp.bfloat16)
     hidden_rows = hidden.reshape(seq_count * shard, width)
     cot_rows = cot_next.reshape(seq_count * shard, width)
     query_left = grad_query.reshape(seq_count * shard, -1)
-    keyval_left = grad_kv.reshape(seq_count * shard, -1)
     attended_rows = attended.reshape(seq_count * shard, -1)
     contract_rows = (((0,), (0,)), ((), ()))
     ctx_count = lax.axis_size("ctx")
     fsdp_count = lax.axis_size("fsdp")
-    term_q, term_kv = (
-        lax.dot_general(hidden_rows, left, contract_rows, preferred_element_type=jnp.float32)
-        for left in (query_left, keyval_left)
+    term_q = lax.dot_general(
+        hidden_rows, query_left, contract_rows, preferred_element_type=jnp.float32
     )
     term_out = 2.0 * lax.dot_general(
         cot_rows, attended_rows, contract_rows, preferred_element_type=jnp.float32
     )
     token_total = seq_count * shard * ctx_count * fsdp_count
-    grad_weights = reduce_terms(
+    grad_weights, grad_kv = reduce_terms(
         term_q.astype(jnp.bfloat16),
-        term_kv.astype(jnp.bfloat16),
         term_out.astype(jnp.bfloat16),
+        hidden_rows,
+        [piece.reshape(seq_count * shard, -1) for piece in pieces],
         1.0 / math.sqrt(token_total),
     )
+    grad_kv = grad_kv.reshape(seq_count, shard, -1)
+    grad_hidden = jnp.einsum("sic,dc->sid", grad_query, full_q, preferred_element_type=jnp.float32)
+    grad_hidden = grad_hidden + jnp.einsum(
+        "sic,dc->sid", grad_kv, full_kv, preferred_element_type=jnp.float32
+    )
+    grad_x = inv_rms * (
+        grad_hidden - normed * jnp.mean(grad_hidden * normed, axis=-1, keepdims=True)
+    )
+    grad_cur = (cot_cur.astype(jnp.float32) + grad_x).astype(jnp.bfloat16)
     return (x_prev, grad_cur, grad_weights)
 
 

time: 208 us -> 185 us (0.89)
  the two profiles are of different devices: /device:TPU:8 before, /device:TPU:0 now
where the time goes in v3:
time: 185 us
  Pallas kernels  146 us (79%)
  starting transfers between devices  12.7 us (7%)
  matrix products  10.2 us (6%)
  waiting for transfers between devices  7.99 us (4%)
  other arithmetic  4.71 us (3%)
  local copies, waits for them, and re-layouts  2.51 us (1%)
    pallas_call x1, Pallas kernels, reduce_terms(): pl.pallas_call(functools.partial(reduce_kernel, ctx_count, fsdp_count, pr...  89.2 us
    pallas_call x1, Pallas kernels, gather_weights(): pl.pallas_call(functools.partial(gather_kernel, count), out_shape=shapes,...  41.4 us
    pallas_call x1, Pallas kernels, attend(): pl.pallas_call(functools.partial(attend_kernel, count - 1), grid=(KEY_VAL...  15.4 us
    ppermute x4, starting transfers between devices, from_behind(): lax.ppermute(value, axis, [(source, source + steps) for source in range(l...  12.7 us
    ppermute x4, waiting for transfers between devices, from_behind(): lax.ppermute(value, axis, [(source, source + steps) for source in range(l...  7.99 us
  transfers between devices with their start and end apart: 4, of which 2 were waited for; matrix products, arithmetic and copies ran while one was open for 1% of the time, Pallas kernels for 0%

profile of v3, /device:TPU:0, one launch (start us, length us, event | category | flops | bytes accessed | tf_op | source)
XLA Modules:
  0.0 185.0 jit_solution(16599968012074696270)
XLA Ops:
  0.6 0.0 copy-start
  0.6 0.0 copy-start.2
  0.7 0.0 copy-start.3
  0.7 1.7 fusion.13
  2.3 1.5 fusion.16.refs_2_
  3.8 41.4 %gather_weights.1 = (bf16[2048,1024]{1,0:T(8,128)(2,1)S(1)}, bf16[2048,512]{1,0:T(8,128)(2,1)S(1)}, bf16[2048,1024]{1,0:T(8,128)(2,1)S(1)}) custom-call(bf16[512,1024]{1,0:T(8,128)(2,1)S(1)} %copy-done.1, bf16[512,512]{1,0:T(8,128)(2,1)S(1)} %copy-done.3, bf16[512,1024]{1,0:T(8,128)(2,1)S(1)} %copy-done.2), custom_call_target="tpu_custom_call" | custom-call | tf_op jit(solution)/shard_map/gather_weights/pallas_call | solution.py:110
  45.3 0.0 copy-start.4
  45.3 0.7 convolution_convert_fusion.2.refs_4_.refs_9_
  46.0 2.6 %collective-permute-start.3 = (bf16[1,256,512]{2,1,0:T(8,128)(2,1)S(1)}, bf16[1,256,512]{2,1,0:T(8,128)(2,1)S(1)}, u32[]{:S(2)}, u32[]{:S(2)}) collective-permute-start(bf16[1,256,512]{2,1,0:T(8,128)(2,1)S(1)} %bitcast.38), channel_id=1, source_target_pairs={{0,4},{4,8},{8,12},{12,16},{16,20},{20,24},{24,28},{1,5},{5,9},{9,... | collective-permute-start | bytes 786440 | tf_op jit(solution)/shard_map/ppermute | solution.py:374
  48.6 3.5 %collective-permute-start.2 = (bf16[1,256,512]{2,1,0:T(8,128)(2,1)S(1)}, bf16[1,256,512]{2,1,0:T(8,128)(2,1)S(1)}, u32[]{:S(2)}, u32[]{:S(2)}) collective-permute-start(bf16[1,256,512]{2,1,0:T(8,128)(2,1)S(1)} %bitcast.39), channel_id=1, source_target_pairs={{0,8},{4,12},{8,16},{12,20},{16,24},{20,28},{1,9},{5,13},{9,17},{1... | collective-permute-start | bytes 786440 | tf_op jit(solution)/shard_map/ppermute | solution.py:374
  52.1 5.3 %collective-permute-start.1 = (bf16[1,256,512]{2,1,0:T(8,128)(2,1)S(1)}, bf16[1,256,512]{2,1,0:T(8,128)(2,1)S(1)}, u32[]{:S(2)}, u32[]{:S(2)}) collective-permute-start(bf16[1,256,512]{2,1,0:T(8,128)(2,1)S(1)} %bitcast.40), channel_id=1, source_target_pairs={{0,12},{4,16},{8,20},{12,24},{16,28},{1,13},{5,17},{9,21},{13,25},... | collective-permute-start | bytes 786440 | tf_op jit(solution)/shard_map/ppermute | solution.py:374
  57.4 1.3 collective-permute-start
  58.7 1.2 convolution_convert_fusion.1.q_ref
  60.0 1.2 fusion.15.g_ref
  61.2 0.0 collective-permute-done.3
  61.3 0.0 collective-permute-done.2
  61.3 2.9 %collective-permute-done.1 = bf16[1,256,512]{2,1,0:T(8,128)(2,1)S(1)} collective-permute-done((bf16[1,256,512]{2,1,0:T(8,128)(2,1)S(1)}, bf16[1,256,512]{2,1,0:T(8,128)(2,1)S(1)}, u32[]{:S(2)}, u32[]{:S(2)}) %collective-permute-start.1) | collective-permute-done | bytes 262176 | tf_op jit(solution)/shard_map/ppermute | solution.py:374
  64.1 5.1 %collective-permute-done = bf16[1,256,512]{2,1,0:T(8,128)(2,1)S(1)} collective-permute-done((bf16[1,256,512]{2,1,0:T(8,128)(2,1)S(1)}, bf16[1,256,512]{2,1,0:T(8,128)(2,1)S(1)}, u32[]{:S(2)}, u32[]{:S(2)}) %collective-permute-start) | collective-permute-done | bytes 262176 | tf_op jit(solution)/shard_map/ppermute | solution.py:374
  69.3 15.4 %attend.1 = (bf16[256,1024]{1,0:T(8,128)(2,1)S(1)}, bf16[256,1024]{1,0:T(8,128)(2,1)S(1)}, bf16[256,512]{1,0:T(8,128)(2,1)S(1)}, bf16[256,512]{1,0:T(8,128)(2,1)...) custom-call(bf16[256,1024]{1,0:T(8,128)(2,1)S(1)} %convolution_convert_fusion.1.q_ref, ...), custom_call_target="tpu_custom_call" | custom-call | flops 3355443200 | bytes 4194304 | tf_op jit(solution)/shard_map/attend/pallas_call | solution.py:466
  84.7 0.0 copy-start.8
  84.7 1.3 fusion.refs_1_
  86.0 0.9 copy-done.5
  86.8 0.3 copy-done.8
  87.1 2.3 %fusion.7 = bf16[1,256,2048]{2,1,0:T(8,128)(2,1)} fusion(bf16[256,1024]{1,0:T(8,128)(2,1)S(1)} %get-tuple-element.18, bf16[2048,1024]{1,0:T(8,128)(2,1)S(1)} %copy-done.5, bf16[1,256,2048]{2,1,0:T(8,128)(2,1)S(1)} %copy-done.8), kind=kOutput, calls=%fused_computation.13 | convolution fusion | flops 1075838976 | bytes 6815744 | tf_op jit(solution)/shard_map/sic,dc->sid/dot_general | solution.py:509
  89.4 1.3 convolution_convert_fusion.refs_0_
  90.7 89.2 %reduce_terms.1 = (f32[64,2560]{1,0:T(8,128)S(1)}, bf16[256,512]{1,0:T(8,128)(2,1)S(1)}) custom-call(bf16[2048,1024]{1,0:T(8,128)(2,1)S(1)} %convolution_convert_fusion.refs_0_, bf16[2048,1024]{1,0:T(8,128)(2,1)S(1)} %fusion.refs_1_, bf16[256,2048]{1,0:T(8,128)(2,1)S(1)} %fusion.16.refs_2_, bf16[256,512]{1,0:T(8,128)(2,1)S(1)} %get-tuple-element.20.refs_3_, ...), custom_call_target="tpu_custom_call" | custom-call | tf_op jit(solution)/shard_map/reduce_terms/pallas_call | solution.py:354
  179.8 0.0 copy-start.6
  179.9 0.7 fusion.19
  180.6 0.5 copy-done.6
  181.1 1.5 fusion.8
  182.6 1.6 fusion.12
  184.1 0.8 copy.15
  (11 shorter events, 0.0 us)
Async XLA Ops:
  0.6 59.4 %copy-start = (bf16[1,256,2048]{2,1,0:T(8,128)(2,1)S(1)}, bf16[1,256,2048]{2,1,0:T(8,128)(2,1)}, u32[]{:S(2)}) copy-start(bf16[1,256,2048]{2,1,0:T(8,128)(2,1)} %param.10) | copy-start | bytes 3145732
  0.6 3.2 %copy-start.2 = (bf16[512,1024]{1,0:T(8,128)(2,1)S(1)}, bf16[512,1024]{1,0:T(8,128)(2,1)}, u32[]{:S(2)}) copy-start(bf16[512,1024]{1,0:T(8,128)(2,1)} %o_in.1) | copy-start | bytes 3145732
  0.7 3.2 %copy-start.3 = (bf16[512,512]{1,0:T(8,128)(2,1)S(1)}, bf16[512,512]{1,0:T(8,128)(2,1)}, u32[]{:S(2)}) copy-start(bf16[512,512]{1,0:T(8,128)(2,1)} %kv_in.1) | copy-start | bytes 1572868
  0.7 3.2 %copy-start.1 = (bf16[512,1024]{1,0:T(8,128)(2,1)S(1)}, bf16[512,1024]{1,0:T(8,128)(2,1)}, u32[]{:S(2)}) copy-start(bf16[512,1024]{1,0:T(8,128)(2,1)} %q_in.1) | copy-start | bytes 3145732
  45.3 14.7 %copy-start.4 = (bf16[2048,1024]{1,0:T(8,128)(2,1)}, bf16[2048,1024]{1,0:T(8,128)(2,1)S(1)}, u32[]{:S(2)}) copy-start(bf16[2048,1024]{1,0:T(8,128)(2,1)S(1)} %get-tuple-element.16) | copy-start | bytes 12582916
  46.0 15.2 %collective-permute-start.3 = (bf16[1,256,512]{2,1,0:T(8,128)(2,1)S(1)}, bf16[1,256,512]{2,1,0:T(8,128)(2,1)S(1)}, u32[]{:S(2)}, u32[]{:S(2)}) collective-permute-start(bf16[1,256,512]{2,1,0:T(8,128)(2,1)S(1)} %bitcast.38), channel_id=1, source_target_pairs={{0,4},{4,8},{8,12},{12,16},{16,20},{20,24},{24,28},{1,5},{5,9},{9,... | collective-permute-start | bytes 786440 | tf_op jit(solution)/shard_map/ppermute | solution.py:374
  48.6 12.6 %collective-permute-start.2 = (bf16[1,256,512]{2,1,0:T(8,128)(2,1)S(1)}, bf16[1,256,512]{2,1,0:T(8,128)(2,1)S(1)}, u32[]{:S(2)}, u32[]{:S(2)}) collective-permute-start(bf16[1,256,512]{2,1,0:T(8,128)(2,1)S(1)} %bitcast.39), channel_id=1, source_target_pairs={{0,8},{4,12},{8,16},{12,20},{16,24},{20,28},{1,9},{5,13},{9,17},{1... | collective-permute-start | bytes 786440 | tf_op jit(solution)/shard_map/ppermute | solution.py:374
  52.1 12.0 %collective-permute-start.1 = (bf16[1,256,512]{2,1,0:T(8,128)(2,1)S(1)}, bf16[1,256,512]{2,1,0:T(8,128)(2,1)S(1)}, u32[]{:S(2)}, u32[]{:S(2)}) collective-permute-start(bf16[1,256,512]{2,1,0:T(8,128)(2,1)S(1)} %bitcast.40), channel_id=1, source_target_pairs={{0,12},{4,16},{8,20},{12,24},{16,28},{1,13},{5,17},{9,21},{13,25},... | collective-permute-start | bytes 786440 | tf_op jit(solution)/shard_map/ppermute | solution.py:374
  57.4 11.8 %collective-permute-start = (bf16[1,256,512]{2,1,0:T(8,128)(2,1)S(1)}, bf16[1,256,512]{2,1,0:T(8,128)(2,1)S(1)}, u32[]{:S(2)}, u32[]{:S(2)}) collective-permute-start(bf16[1,256,512]{2,1,0:T(8,128)(2,1)S(1)} %bitcast.41), channel_id=1, source_target_pairs={{0,16},{4,20},{8,24},{12,28},{1,17},{5,21},{9,25},{13,29},{2,18},{... | collective-permute-start | bytes 786440 | tf_op jit(solution)/shard_map/ppermute | solution.py:374
  84.6 2.2 %copy-start.5 = (bf16[2048,1024]{1,0:T(8,128)(2,1)S(1)}, bf16[2048,1024]{1,0:T(8,128)(2,1)}, u32[]{:S(2)}) copy-start(bf16[2048,1024]{1,0:T(8,128)(2,1)} %copy-done.4) | copy-start | bytes 12582916
  84.7 2.5 %copy-start.8 = (bf16[1,256,2048]{2,1,0:T(8,128)(2,1)S(1)}, bf16[1,256,2048]{2,1,0:T(8,128)(2,1)}, u32[]{:S(2)}) copy-start(bf16[1,256,2048]{2,1,0:T(8,128)(2,1)} %param.8) | copy-start | bytes 3145732
  179.8 1.2 copy-start.6
  181.1 1.5 copy-start.7

commit v4 on v3

--- a/solution.py
+++ b/solution.py
@@ -368,6 +368,83 @@
     )(term_q, term_o, hidden, *pieces)
 
 
+def share_kernel(ctx_count, kv_ref, hop1, hop2, hop3, hop4, send_sem, recv_sem):
+    ctx_at = lax.axis_index("ctx")
+    fsdp_at = lax.axis_index("fsdp")
+    odd = lax.rem(ctx_at, 2)
+    peer = ctx_at + 1 - 2 * odd
+    slots = (hop1, hop2, hop3, hop4)
+
+    barrier = pltpu.get_barrier_semaphore()
+    pl.semaphore_signal(barrier, inc=1, device_id=(peer, fsdp_at), device_id_type=MESH)
+
+    @pl.when(ctx_at >= 2)
+    def _():
+        pl.semaphore_signal(barrier, inc=1, device_id=(ctx_at - 2, fsdp_at), device_id_type=MESH)
+
+    pl.semaphore_wait(barrier, 1 + jnp.minimum((ctx_count - 1 - ctx_at) // 2, 1))
+
+    def copy(src, hop, slot, target):
+        return pltpu.make_async_remote_copy(
+            src_ref=src, dst_ref=slots[hop - 1],
+            send_sem=send_sem.at[slot], recv_sem=recv_sem.at[hop - 1],
+            device_id=(target, fsdp_at), device_id_type=MESH,
+        )
+
+    onward = ctx_at + 2 < ctx_count
+    plan = (
+        (onward, kv_ref, 2, 0, ctx_at + 2),
+        (odd == 0, kv_ref, 1, 1, peer),
+        ((ctx_at >= 2) & onward, hop2, 4, 2, ctx_at + 2),
+        ((ctx_at >= 2) & (odd == 0), hop2, 3, 3, peer),
+        ((ctx_at >= 2) & (odd == 1), hop2, 1, 4, peer),
+        ((ctx_at >= 4) & (odd == 1), hop4, 3, 5, peer),
+    )
+
+    def begin(entries):
+        for valid, src, hop, slot, target in entries:
+
+            @pl.when(valid)
+            def _():
+                copy(src, hop, slot, target).start()
+
+    def arrive(hop):
+        @pl.when(ctx_at >= hop)
+        def _():
+            copy(kv_ref, hop, 0, peer).wait_recv()
+
+    begin(plan[:2])
+    for hop in range(1, 5):
+
+        @pl.when(ctx_at < hop)
+        def _():
+            slots[hop - 1][...] = jnp.zeros_like(slots[hop - 1])
+
+    arrive(2)
+    begin(plan[2:5])
+    arrive(4)
+    begin(plan[5:])
+    arrive(1)
+    arrive(3)
+    for valid, src, hop, slot, target in plan:
+
+        @pl.when(valid)
+        def _():
+            copy(src, hop, slot, target).wait_send()
+
+
+def share_keys(rows):
+    return pl.pallas_call(
+        functools.partial(share_kernel, lax.axis_size("ctx")),
+        out_shape=[jax.ShapeDtypeStruct(rows.shape, rows.dtype)] * 4,
+        in_specs=[pl.BlockSpec(memory_space=pltpu.VMEM)],
+        out_specs=[pl.BlockSpec(memory_space=pltpu.VMEM)] * 4,
+        scratch_shapes=[pltpu.SemaphoreType.DMA((6,)), pltpu.SemaphoreType.DMA((4,))],
+        compiler_params=pltpu.CompilerParams(collective_id=2, has_side_effects=True),
+        name="share_keys",
+    )(rows)
+
+
 def from_behind(value, axis, steps):
     count = lax.axis_size(axis)
     leading, last = (max(0, -steps), min(count, count - steps))
@@ -498,9 +575,13 @@
     grad_attn = (
         2.0 * jnp.einsum("sid,dc->sic", cot_next, full_out, preferred_element_type=jnp.float32)
     ).astype(jnp.bfloat16)
-    earlier = []
-    for hop in range(1, preds + 1):
-        earlier.append(from_behind(key_value_pairs, "ctx", hop))
+    if preds == 4 and lax.axis_size("ctx") % 2 == 0:
+        pair_rows = key_value_pairs.reshape(seq_count * shard, -1)
+        earlier = [block.reshape(key_value_pairs.shape) for block in share_keys(pair_rows)]
+    else:
+        earlier = []
+        for hop in range(1, preds + 1):
+            earlier.append(from_behind(key_value_pairs, "ctx", hop))
     results = []
     for seq in range(seq_count):
         window = [block[seq] for block in earlier[::-1]] + [key_value_pairs[seq]]

time: 185 us -> 178 us (0.962)
  starting transfers between devices: 12.7 us -> 0 us
  Pallas kernels: 146 us -> 154 us
  waiting for transfers between devices: 7.99 us -> 0 us
  local copies, waits for them, and re-layouts: 2.51 us -> 6.98 us
    ppermute x4 -> x0, starting transfers between devices: 12.7 us -> none  [from_behind(): lax.ppermute(value, axis, [(source, source + steps) for source in range(l...]
    pallas_call x0 -> x1, Pallas kernels: none -> 9.78 us  [share_keys(): pl.pallas_call(functools.partial(share_kernel, lax.axis_size('ctx')), out...]
    ppermute x4 -> x0, waiting for transfers between devices: 7.99 us -> none  [from_behind(): lax.ppermute(value, axis, [(source, source + steps) for source in range(l...]
    unnamed x19 -> x37, local copies, waits for them, and re-layouts: 2.51 us -> 6.98 us
    pallas_call x1, Pallas kernels: 89.2 us -> 86.9 us  [reduce_terms(): pl.pallas_call(functools.partial(reduce_kernel, ctx_count, fsdp_count, pr...]
  transfers between devices with their start and end apart: 4 -> 0, of which waited for: 2 -> 0; matrix products, arithmetic and copies ran while one was open for 1% -> 0% of each run, Pallas kernels for 0% -> 0%
where the time goes in v4:
time: 178 us; the launch traced here: 177 us
  Pallas kernels  154 us (87%)
  matrix products  11.4 us (6%)
  local copies, waits for them, and re-layouts  6.98 us (4%)
  other arithmetic  4.71 us (3%)
    pallas_call x1, Pallas kernels, reduce_terms(): pl.pallas_call(functools.partial(reduce_kernel, ctx_count, fsdp_count, pr...  86.9 us
    pallas_call x1, Pallas kernels, gather_weights(): pl.pallas_call(functools.partial(gather_kernel, count), out_shape=shapes,...  41.4 us
    pallas_call x1, Pallas kernels, attend(): pl.pallas_call(functools.partial(attend_kernel, count - 1), grid=(KEY_VAL...  15.4 us
    pallas_call x1, Pallas kernels, share_keys(): pl.pallas_call(functools.partial(share_kernel, lax.axis_size('ctx')), out...  9.78 us
    unnamed x37, local copies, waits for them, and re-layouts  6.98 us

profile of v4, /device:TPU:0, one launch (start us, length us, event | category | flops | bytes accessed | tf_op | source)
XLA Modules:
  0.0 177.5 jit_solution(10649568415104142811)
XLA Ops:
  0.6 0.0 copy-start
  0.7 1.7 fusion.13
  2.3 1.5 fusion.16.refs_2_
  3.8 41.4 %gather_weights.1 = (bf16[2048,1024]{1,0:T(8,128)(2,1)S(1)}, bf16[2048,512]{1,0:T(8,128)(2,1)S(1)}, bf16[2048,1024]{1,0:T(8,128)(2,1)S(1)}) custom-call(bf16[512,1024]{1,0:T(8,128)(2,1)S(1)} %copy-done.3, bf16[512,512]{1,0:T(8,128)(2,1)S(1)} %copy-done.5, bf16[512,1024]{1,0:T(8,128)(2,1)S(1)} %copy-done.4), custom_call_target="tpu_custom_call" | custom-call | tf_op jit(solution)/shard_map/gather_weights/pallas_call | solution.py:110
  45.3 1.9 %convolution_convert_fusion.2.kv_ref.refs_4_.refs_9_ = bf16[256,512]{1,0:T(8,128)(2,1)} fusion(bf16[256,2048]{1,0:T(8,128)(2,1)S(1)} %fusion.16.refs_2_, bf16[2048,512]{1,0:T(8,128)(2,1)S(1)} %get-tuple-element.21), kind=kOutput, calls=%fused_computation.24 | convolution fusion | flops 537001984 | bytes 3407872 | tf_op jit(solution)/shard_map/sid,dc->sic/dot_general | solution.py:572
  47.2 1.2 convolution_convert_fusion.1.q_ref
  48.5 0.8 copy-done.9
  49.3 1.2 fusion.15.g_ref
  50.5 9.8 %share_keys.1 = (bf16[256,512]{1,0:T(8,128)(2,1)}, bf16[256,512]{1,0:T(8,128)(2,1)}, bf16[256,512]{1,0:T(8,128)(2,1)}, bf16[256,512]{1,0:T(8,128)(2,1)}) custom-call(bf16[256,512]{1,0:T(8,128)(2,1)} %convolution_convert_fusion.2.kv_ref.refs_4_.refs_9_), custom_call_target="tpu_custom_call" | custom-call | tf_op jit(solution)/shard_map/share_keys/pallas_call | solution.py:437
  60.3 0.9 copy-done.11
  61.3 0.9 copy-done.12
  62.2 0.9 copy-done.13
  63.2 0.9 copy-done.14
  64.1 15.4 %attend.1 = (bf16[256,1024]{1,0:T(8,128)(2,1)S(1)}, bf16[256,1024]{1,0:T(8,128)(2,1)S(1)}, bf16[256,512]{1,0:T(8,128)(2,1)S(1)}, bf16[256,512]{1,0:T(8,128)(2,1)...) custom-call(bf16[256,1024]{1,0:T(8,128)(2,1)S(1)} %convolution_convert_fusion.1.q_ref, ...), custom_call_target="tpu_custom_call" | custom-call | flops 3355443200 | bytes 4194304 | tf_op jit(solution)/shard_map/attend/pallas_call | solution.py:543
  79.5 0.0 copy-done.10
  79.5 0.0 copy-start.8
  79.6 0.0 copy-start.17
  79.6 1.3 fusion.19
  80.9 0.9 copy-done.8
  81.7 0.3 copy-done.17
  82.0 2.3 %fusion.7 = bf16[1,256,2048]{2,1,0:T(8,128)(2,1)} fusion(bf16[256,1024]{1,0:T(8,128)(2,1)S(1)} %get-tuple-element.26, bf16[2048,1024]{1,0:T(8,128)(2,1)S(1)} %copy-done.8, bf16[1,256,2048]{2,1,0:T(8,128)(2,1)S(1)} %copy-done.17), kind=kOutput, calls=%fused_computation.13 | convolution fusion | flops 1075838976 | bytes 6815744 | tf_op jit(solution)/shard_map/sic,dc->sid/dot_general | solution.py:590
  84.3 1.3 fusion.refs_1_
  85.6 1.3 convolution_convert_fusion.refs_0_
  86.9 0.0 copy-start.2
  86.9 0.0 copy-start.15
  86.9 86.9 %reduce_terms.1 = (f32[64,2560]{1,0:T(8,128)S(1)}, bf16[256,512]{1,0:T(8,128)(2,1)S(1)}) custom-call(bf16[2048,1024]{1,0:T(8,128)(2,1)S(1)} %convolution_convert_fusion.refs_0_, bf16[2048,1024]{1,0:T(8,128)(2,1)S(1)} %fusion.refs_1_, bf16[256,2048]{1,0:T(8,128)(2,1)S(1)} %fusion.16.refs_2_, bf16[256,512]{1,0:T(8,128)(2,1)S(1)} %get-tuple-element.28.refs_3_, ...), custom_call_target="tpu_custom_call" | custom-call | tf_op jit(solution)/shard_map/reduce_terms/pallas_call | solution.py:354
  173.8 0.0 copy-done.2
  173.9 0.0 copy-start.16
  173.9 0.9 fusion.8
  174.7 0.4 copy-done.16
  175.1 1.6 fusion.12
  176.7 0.8 copy.15
  (22 shorter events, 0.1 us)
Async XLA Ops:
  0.6 48.7 %copy-start = (bf16[1,256,2048]{2,1,0:T(8,128)(2,1)S(1)}, bf16[1,256,2048]{2,1,0:T(8,128)(2,1)}, u32[]{:S(2)}) copy-start(bf16[1,256,2048]{2,1,0:T(8,128)(2,1)} %param.10) | copy-start | bytes 3145732
  0.6 3.2 %copy-start.4 = (bf16[512,1024]{1,0:T(8,128)(2,1)S(1)}, bf16[512,1024]{1,0:T(8,128)(2,1)}, u32[]{:S(2)}) copy-start(bf16[512,1024]{1,0:T(8,128)(2,1)} %o_in.1) | copy-start | bytes 3145732
  0.7 3.2 %copy-start.5 = (bf16[512,512]{1,0:T(8,128)(2,1)S(1)}, bf16[512,512]{1,0:T(8,128)(2,1)}, u32[]{:S(2)}) copy-start(bf16[512,512]{1,0:T(8,128)(2,1)} %kv_in.1) | copy-start | bytes 1572868
  0.7 3.2 %copy-start.3 = (bf16[512,1024]{1,0:T(8,128)(2,1)S(1)}, bf16[512,1024]{1,0:T(8,128)(2,1)}, u32[]{:S(2)}) copy-start(bf16[512,1024]{1,0:T(8,128)(2,1)} %q_in.1) | copy-start | bytes 3145732
  45.3 3.2 %copy-start.1 = (bf16[2048,512]{1,0:T(8,128)(2,1)}, bf16[2048,512]{1,0:T(8,128)(2,1)S(1)}, u32[]{:S(2)}) copy-start(bf16[2048,512]{1,0:T(8,128)(2,1)S(1)} %get-tuple-element.21) | copy-start | bytes 6291460
  45.3 3.2 %copy-start.7 = (bf16[2048,1024]{1,0:T(8,128)(2,1)}, bf16[2048,1024]{1,0:T(8,128)(2,1)S(1)}, u32[]{:S(2)}) copy-start(bf16[2048,1024]{1,0:T(8,128)(2,1)S(1)} %get-tuple-element.20) | copy-start | bytes 12582916
  45.3 4.0 %copy-start.9 = (bf16[2048,1024]{1,0:T(8,128)(2,1)}, bf16[2048,1024]{1,0:T(8,128)(2,1)S(1)}, u32[]{:S(2)}) copy-start(bf16[2048,1024]{1,0:T(8,128)(2,1)S(1)} %get-tuple-element.19) | copy-start | bytes 12582916
  49.3 11.0 %copy-start.6 = (bf16[256,512]{1,0:T(8,128)(2,1)S(1)}, bf16[256,512]{1,0:T(8,128)(2,1)}, u32[]{:S(2)}) copy-start(bf16[256,512]{1,0:T(8,128)(2,1)} %convolution_convert_fusion.2.kv_ref.refs_4_.refs_9_) | copy-start | bytes 786436
  60.3 1.0 copy-start.11
  61.3 0.9 copy-start.12
  62.2 0.9 copy-start.13
  63.2 0.9 copy-start.14
  64.1 15.4 %copy-start.10 = (bf16[2048,1024]{1,0:T(8,128)(2,1)S(1)}, bf16[2048,1024]{1,0:T(8,128)(2,1)}, u32[]{:S(2)}) copy-start(bf16[2048,1024]{1,0:T(8,128)(2,1)} %copy-done.9) | copy-start | bytes 12582916
  79.5 2.2 %copy-start.8 = (bf16[2048,1024]{1,0:T(8,128)(2,1)S(1)}, bf16[2048,1024]{1,0:T(8,128)(2,1)}, u32[]{:S(2)}) copy-start(bf16[2048,1024]{1,0:T(8,128)(2,1)} %copy-done.7) | copy-start | bytes 12582916
  79.6 2.5 %copy-start.17 = (bf16[1,256,2048]{2,1,0:T(8,128)(2,1)S(1)}, bf16[1,256,2048]{2,1,0:T(8,128)(2,1)}, u32[]{:S(2)}) copy-start(bf16[1,256,2048]{2,1,0:T(8,128)(2,1)} %param.8) | copy-start | bytes 3145732
  86.9 87.0 %copy-start.2 = (bf16[2048,512]{1,0:T(8,128)(2,1)S(1)}, bf16[2048,512]{1,0:T(8,128)(2,1)}, u32[]{:S(2)}) copy-start(bf16[2048,512]{1,0:T(8,128)(2,1)} %copy-done.1) | copy-start | bytes 6291460
  86.9 87.0 %copy-start.15 = (bf16[1,256,2048]{2,1,0:T(8,128)(2,1)S(1)}, bf16[1,256,2048]{2,1,0:T(8,128)(2,1)}, u32[]{:S(2)}) copy-start(bf16[1,256,2048]{2,1,0:T(8,128)(2,1)} %param.7) | copy-start | bytes 3145732
  173.9 1.2 copy-start.16
